TPU v7x, 256 devices: a whole 4x4x8 slice. The times are simulated.
256 devices in a mesh: mp: 4 (over y), nodes: 64 (over z, x, core).
Axes of the slice: x: 4, y: 4, z: 8, core: 2. Of those that a mesh axis runs over, the one named last changes fastest.
Arguments:
- grid_latent: float32 [131072, 512], P('nodes'), may hold values from -6 to 6
- mesh_latent: float32 [8192, 512], P('nodes'), may hold values from -250 to 250
- enc_grid_w: float32 [512, 512], P(None, 'mp'), may hold values from -0.25 to 0.25
- enc_mesh_w: float32 [512, 512], P(None, 'mp'), may hold values from -0.25 to 0.25
- enc_out_w: float32 [512, 512], P('mp'), may hold values from -0.25 to 0.25
- block_gain: float32 [512], replicated, may hold values from 0.5 to 1.5
- query_w: float32 [512, 512], P(None, 'mp'), may hold values from -1 to 1
- key_w: float32 [512, 512], P(None, 'mp'), may hold values from -1 to 1
- value_w: float32 [512, 512], P(None, 'mp'), may hold values from -0.25 to 0.25
- out_w: float32 [512, 512], P('mp'), may hold values from -0.25 to 0.25
- up_w: float32 [512, 2048], P(None, 'mp'), may hold values from -0.25 to 0.25
- down_w: float32 [2048, 512], P('mp'), may hold values from -0.125 to 0.125
- dec_gain: float32 [512], replicated, may hold values from 0.5 to 1.5
- dec_grid_w: float32 [512, 512], P(None, 'mp'), may hold values from -0.25 to 0.25
- dec_mesh_w: float32 [512, 512], P(None, 'mp'), may hold values from -0.25 to 0.25
- dec_out_w: float32 [512, 512], P('mp'), may hold values from -0.25 to 0.25
- neighbor_blocks: int32 [64, 16], replicated, may hold values from 0 to 63, as said below
- enc_tiles: int32 [2048, 2], P('nodes'), may hold values from -1 to 1023, as said below
- enc_edges: int32 [2048, 2, 128], P('nodes'), may hold values from 0 to 127
- dec_tiles: int32 [3072, 2], P('nodes'), may hold values from 0 to 1023, as said below
- dec_edges: int32 [3072, 2, 128], P('nodes'), may hold values from 0 to 127
Outputs:
- grid_out: float32 [131072, 512], P('nodes', 'mp')
Inputs may be any that keep to these rules, and one draw needn't show every extreme that they name: `neighbor_blocks`: rows i * 1 to (i + 1) - 1 are the query blocks of index i of nodes; among all entries of those rows, the blocks of any one index j of nodes (ids j * 1 to (j + 1) - 1) are named at most 1 times, and for every i some j is named exactly 1 times. Entries may repeat. `enc_tiles`: tile slots i * 32 to (i + 1) * 32 - 1 belong to index i of nodes; a live tile names a grid block and a mesh block both of index i; an unused slot holds -1 in both columns; on each index the live slots come first, their number differs between indices, and some index has all 32 slots live. `dec_tiles`: tiles i * 48 to (i + 1) * 48 - 1 belong to index i of nodes; each names a grid block of index i and a mesh block of index i - 1, i or i + 1 of nodes (counted around the axis).
All inputs are finite; a program needn't handle non-finite values.
Results may differ from a plain program's by a relative error of at most 0.000098.
Values sent between devices are 32-bit elements; how exact they have to be, the bound alone decides.
A program may use at most 128 MiB of HBM per device.

v0:
```python
import math

import jax
import jax.numpy as jnp
from jax import lax
from jax.sharding import PartitionSpec as P

HEAD_DIM = 128
NODE_BLOCK = 128


FULL_PRECISION = lax.Precision.HIGHEST


def copy_for_each(shard, axis):
    devices = lax.axis_size(axis)
    return lax.all_to_all(
        jnp.broadcast_to(shard[None], (devices, *shard.shape)), axis, 0, 0, tiled=True
    )


def taken_together(shard, axis):
    everything = copy_for_each(shard, axis)
    return jnp.sum(everything, axis=0)


def padded(shard, sides, width):
    for axis, dim in sides:
        devices, length = (lax.axis_size(axis), shard.shape[dim])
        up = [(i, (i + 1) % devices) for i in range(devices)]
        down = [(j, i) for i, j in up]
        last = lax.slice_in_dim(shard, length - width, length, axis=dim)
        initial = lax.slice_in_dim(shard, 0, width, axis=dim)
        before = lax.ppermute(last, axis, up)
        after = lax.ppermute(initial, axis, down)
        shard = jnp.concatenate([before, shard, after], axis=dim)
    return shard


def product(matrix, weight):
    return jnp.dot(matrix, weight, precision=FULL_PRECISION, preferred_element_type=jnp.float32)


def layer_norm(inputs, scales):
    centre = jnp.mean(inputs, axis=-1, keepdims=True)
    shifted = inputs - centre
    spread = jnp.mean(shifted * shifted, axis=-1, keepdims=True)
    return shifted * lax.rsqrt(spread + 1e-05) * scales


def edge_pass(
    source_side, target_side, source_block, target_block, edge_ids, tile_live, target_blocks
):
    source = source_block[:, None] * NODE_BLOCK + edge_ids[:, 0, :]
    target = target_block[:, None] * NODE_BLOCK + edge_ids[:, 1, :]
    message = jax.nn.silu(source_side[source] + target_side[target]) * tile_live[:, None, None]
    within = (edge_ids[:, 1, :][:, None, :] == jnp.arange(NODE_BLOCK)[None, :, None]).astype(
        jnp.float32
    )
    tile_sums = jnp.einsum("tne,teh->tnh", within, message, precision=FULL_PRECISION)
    placing = (target_block[None, :] == jnp.arange(target_blocks)[:, None]).astype(jnp.float32)
    summed = jnp.einsum("bt,tnh->bnh", placing, tile_sums, precision=FULL_PRECISION)
    return summed.reshape(target_blocks * NODE_BLOCK, -1)


def per_device(
    grid_latent,
    mesh_latent,
    enc_grid_w,
    enc_mesh_w,
    enc_out_w,
    block_gain,
    query_w,
    key_w,
    value_w,
    out_w,
    up_w,
    down_w,
    dec_gain,
    dec_grid_w,
    dec_mesh_w,
    dec_out_w,
    neighbor_blocks,
    enc_tiles,
    enc_edges,
    dec_tiles,
    dec_edges,
):
    me_node = lax.axis_index("nodes")
    nodes_count = lax.axis_size("nodes")
    grid_rows = grid_latent.shape[0]
    node_rows = mesh_latent.shape[0]
    grid_blocks = grid_rows // NODE_BLOCK
    node_blocks = node_rows // NODE_BLOCK
    grid_enc = product(grid_latent, enc_grid_w)
    mesh_enc = product(mesh_latent, enc_mesh_w)
    tile_live = enc_tiles[:, 0] >= 0
    source_block = jnp.where(tile_live, enc_tiles[:, 0] - me_node * grid_blocks, 0)
    target_block = jnp.where(tile_live, enc_tiles[:, 1] - me_node * node_blocks, 0)
    enc_agg = edge_pass(
        grid_enc,
        mesh_enc,
        source_block,
        target_block,
        enc_edges,
        tile_live.astype(jnp.float32),
        node_blocks,
    )
    enc_total = taken_together(product(enc_agg, enc_out_w), "mp")
    mesh_one = mesh_latent + enc_total
    normed = layer_norm(mesh_one, block_gain)
    queries = product(normed, query_w)
    key_rows = product(normed, key_w)
    value_rows = product(normed, value_w)
    head_cols = queries.shape[1]
    heads_here = head_cols // HEAD_DIM
    key_values = jnp.concatenate([key_rows, value_rows], axis=1)
    query_blocks = queries.reshape(node_blocks, NODE_BLOCK, heads_here, HEAD_DIM)
    own_lists = lax.dynamic_slice_in_dim(neighbor_blocks, me_node * node_blocks, node_blocks, 0)
    key_piece = lax.all_gather(key_values, "nodes", axis=0, tiled=True)
    running_max = jnp.full((node_blocks, heads_here, NODE_BLOCK), -1e30, jnp.float32)
    row_count = key_piece.shape[0]
    piece_block = jnp.arange(row_count) // NODE_BLOCK
    repeats = jnp.sum(
        (own_lists[:, :, None] == piece_block[None, None, :]).astype(jnp.float32), axis=1
    )
    near_keys = key_piece[:, :head_cols].reshape(row_count, heads_here, HEAD_DIM)
    near_values = key_piece[:, head_cols:].reshape(row_count, heads_here, HEAD_DIM)
    scores = jnp.einsum(
        "bqhd,khd->bhqk", query_blocks, near_keys, precision=FULL_PRECISION
    ) / math.sqrt(HEAD_DIM)
    scores = jnp.where((repeats > 0)[:, None, None, :], scores, -1e30)
    new_max = jnp.maximum(running_max, jnp.max(scores, axis=-1))
    weights = jnp.exp(scores - new_max[..., None]) * repeats[:, None, None, :]
    running_sum = jnp.sum(weights, axis=-1)
    running_out = jnp.einsum("bhqk,khd->bhqd", weights, near_values, precision=FULL_PRECISION)
    running_max, running_sum, running_out = (new_max, running_sum, running_out)
    attended = (
        (running_out / running_sum[..., None]).transpose(0, 2, 1, 3).reshape(node_rows, head_cols)
    )
    hidden = jax.nn.silu(product(normed, up_w))
    block_total = taken_together(product(attended, out_w) + product(hidden, down_w), "mp")
    mesh_two = mesh_one + block_total
    mesh_normed = layer_norm(mesh_two, dec_gain)
    all_blocks = node_blocks * nodes_count
    dec_source = (dec_tiles[:, 0] - (me_node - 1) * node_blocks) % all_blocks
    dec_target = dec_tiles[:, 1] - me_node * grid_blocks
    mesh_dec = product(mesh_normed, dec_mesh_w)
    grid_dec = product(grid_latent, dec_grid_w)
    beside_all = padded(mesh_dec, (("nodes", 0),), node_rows)
    every_tile = jnp.ones((dec_tiles.shape[0],), jnp.float32)
    dec_agg = edge_pass(
        beside_all, grid_dec, dec_source, dec_target, dec_edges, every_tile, grid_blocks
    )
    decoded = lax.psum_scatter(product(dec_agg, dec_out_w), "mp", scatter_dimension=1, tiled=True)
    share_cols = decoded.shape[1]
    grid_share = lax.dynamic_slice_in_dim(
        grid_latent, lax.axis_index("mp") * share_cols, share_cols, 1
    )
    return grid_share + decoded


def solution(mesh):
    in_specs = (
        P("nodes", None),
        P("nodes", None),
        P(None, "mp"),
        P(None, "mp"),
        P("mp", None),
        P(),
        P(None, "mp"),
        P(None, "mp"),
        P(None, "mp"),
        P("mp", None),
        P(None, "mp"),
        P("mp", None),
        P(),
        P(None, "mp"),
        P(None, "mp"),
        P("mp", None),
        P(),
        P("nodes", None),
        P("nodes", None, None),
        P("nodes", None),
        P("nodes", None, None),
    )
    out_specs = P("nodes", "mp")
    return jax.shard_map(
        per_device, mesh=mesh, in_specs=in_specs, out_specs=out_specs, check_vma=False
    )
```

profile of v0, /device:TPU:3, one launch (start us, length us, event | category | flops | bytes accessed | tf_op | source)
XLA Modules:
  0.0 319.4 jit_solution(5665436345619726725)
XLA Ops:
  8.9 5.2 %fusion.94 = f32[2048,128]{1,0:T(8,128)S(1)} fusion(f32[2048,512]{1,0:T(8,128)} %param.21, f32[512,128]{1,0:T(8,128)} %param.23), kind=kOutput, calls=%fused_computation.123 | convolution fusion | flops 1610612736 | bytes 5505024 | tf_op jit(solution)/shard_map/dot_general | solution.py:41
  14.3 14.1 %gather_fusion = f32[4096,128]{1,0:T(8,128)} fusion(f32[2048,128]{1,0:T(8,128)S(1)} %fusion.94, s32[4096]{0:T(1024)S(1)} %get-tuple-element.20), kind=kCustom, calls=%fused_computation | custom fusion | bytes 4210688 | tf_op jit(solution)/shard_map/gather | solution.py:56
  28.8 14.1 %gather_fusion.1 = f32[4096,128]{1,0:T(8,128)} fusion(f32[128,128]{1,0:T(8,128)S(1)} %fusion.95, s32[4096]{0:T(1024)S(1)} %get-tuple-element.21), kind=kCustom, calls=%fused_computation.1 | custom fusion | bytes 4210688 | tf_op jit(solution)/shard_map/gather | solution.py:56
  42.9 1.8 add.221
  44.7 1.9 fusion.19
  46.6 2.0 fusion.15
  49.1 18.2 %all_to_all.10 = f32[4,128,512]{2,1,0:T(8,128)S(1)} all-to-all(f32[4,128,512]{2,1,0:T(8,128)S(1)} %broadcast_in_dim.17), channel_id=1, replica_groups=mesh['mp'=4,'nodes'=64] {'mp'}, dimensions={0} | all-to-all | bytes 2097152 | tf_op jit(solution)/shard_map/all_to_all | solution.py:17
  68.7 1.6 fusion.87
  76.0 85.4 %all-gather.2.cloned.1.call-done = f32[8192,256]{0,1:T(8,128)} async-done(((f32[128,256]{0,1:T(8,128)}), f32[8192,256]{0,1:T(8,128)}) %all-gather.2.cloned.1.call-update) | async-done | bytes 8388624 | tf_op jit(solution)/shard_map/all_gather | solution.py:120
  161.3 10.2 %fusion.92 = (f32[128]{0:T(128)S(1)}, f32[1,8192,1,128]{3,1,2,0:T(8,128)S(1)}) fusion(f32[128,128]{1,0:T(8,128)S(1)} %fusion.85, f32[8192,256]{0,1:T(8,128)} %all-gather.2.cloned.1.call-done, pred[8192]{0:T(1024)(128)(4,1)S(1)} %broadcast_compare_fusion), kind=kOutput, calls=%fused_computation.121 | convolution fusion | flops 1613758336 | bytes 8462848 | tf_op jit(solution)/shard_map/bqhd,khd->bhqk/dot_general | solution.py:129
  171.5 3.5 %fusion.6 = f32[128]{0:T(128)S(1)} fusion(f32[1,8192,1,128]{3,1,2,0:T(8,128)S(1)} %get-tuple-element.19, f32[8192]{0:T(1024)S(1)} %convert_reduce_fusion, f32[128]{0:T(128)S(1)} %broadcast_maximum_fusion), kind=kLoop, calls=%fused_computation.12 | loop fusion | flops 3145600 | bytes 4228096 | tf_op jit(solution)/shard_map/reduce_sum | solution.py:135
  175.0 5.0 %fusion.38 = f32[128,128]{0,1:T(8,128)S(1)} fusion(f32[1,8192,1,128]{3,1,2,0:T(8,128)S(1)} %get-tuple-element.19, f32[8192]{0:T(1024)S(1)} %convert_reduce_fusion, f32[128]{0:T(128)S(1)} %broadcast_maximum_fusion, f32[8192,256]{0,1:T(8,128)S(1)} %copy-done.1, f32[128]{0:T(128)S(1)} %fusion.6), kind=kOutput, calls=%fused_computation.39 | convolution fusion | flops 1612726272 | bytes 8487936 | tf_op jit(solution)/shard_map/bhqk,khd->bhqd/dot_general | solution.py:136
  181.6 4.0 %all-to-all-start.1 = ((f32[4,128,512]{2,1,0:T(8,128)}), f32[4,128,512]{2,1,0:T(8,128)S(1)}, u32[]{:S(2)}, u32[]{:S(2)}) async-start(f32[4,128,512]{2,1,0:T(8,128)} %broadcast_in_dim.21), calls=%async_computation.1 | async-start | bytes 2097152 | tf_op jit(solution)/shard_map/all_to_all | solution.py:17
  185.7 5.2 %fusion.97 = f32[2048,128]{1,0:T(8,128)S(1)} fusion(f32[2048,512]{1,0:T(8,128)} %param.21, f32[512,128]{1,0:T(8,128)} %param.34), kind=kOutput, calls=%fused_computation.126 | convolution fusion | flops 1610612736 | bytes 5505024 | tf_op jit(solution)/shard_map/dot_general | solution.py:41
  190.9 9.3 %all-to-all-done.1 = f32[4,128,512]{2,1,0:T(8,128)S(1)} async-done(((f32[4,128,512]{2,1,0:T(8,128)}), f32[4,128,512]{2,1,0:T(8,128)S(1)}, u32[]{:S(2)}, u32[]{:S(2)}) %all-to-all-start.1) | async-done | bytes 1048608 | tf_op jit(solution)/shard_map/all_to_all | solution.py:17
  203.7 2.8 collective-permute-start
  206.7 20.9 %gather_fusion.3 = f32[6144,128]{1,0:T(8,128)} fusion(f32[2048,128]{1,0:T(8,128)S(1)} %fusion.97, s32[6144]{0:T(1024)S(1)} %get-tuple-element.23), kind=kCustom, calls=%fused_computation.3 | custom fusion | bytes 6316032 | tf_op jit(solution)/shard_map/gather | solution.py:56
  227.6 20.9 %gather_fusion.2 = f32[6144,128]{1,0:T(8,128)} fusion(f32[384,128]{1,0:T(8,128)S(1)} %pad_maximum_fusion, s32[6144]{0:T(1024)S(1)} %get-tuple-element.22), kind=kCustom, calls=%fused_computation.2 | custom fusion | bytes 6316032 | tf_op jit(solution)/shard_map/gather | solution.py:56
  248.5 3.2 add.222
  251.7 2.9 fusion.9
  254.7 2.9 fusion.7
  258.0 4.9 %fusion.98 = f32[2048,512]{1,0:T(8,128)} fusion(f32[2048,128]{1,0:T(8,128)S(1)} %bitcast.97, f32[128,512]{1,0:T(8,128)S(1)} %copy-done.8), kind=kOutput, calls=%fused_computation.127 | convolution fusion | flops 1610612736 | bytes 5505024 | tf_op jit(solution)/shard_map/dot_general | solution.py:41
  262.9 47.0 %reduce-scatter.2.cloned.1.call-done = f32[2048,128]{1,0:T(8,128)} async-done(((f32[2048,512]{1,0:T(8,128)}), f32[2048,128]{1,0:T(8,128)}) %reduce-scatter.2.cloned.1.call-update) | async-done | bytes 1048592 | tf_op jit(solution)/shard_map/reduce_scatter | solution.py:155
  309.9 2.6 dynamic-slice_add_fusion
  (72 shorter events, 15.8 us)
Async XLA Ops:
  6.5 67.9 %copy-start = (f32[512,512]{1,0:T(8,128)S(1)}, f32[512,512]{1,0:T(8,128)}, u32[]{:S(2)}) copy-start(f32[512,512]{1,0:T(8,128)} %param.31) | copy-start | bytes 3145732
  6.5 154.8 %all-gather.2.cloned.1.call-start = ((), (), s32[]{:S(2)}) async-start(), calls=%async_computation.3 | async-start | bytes 8519680 | tf_op jit(solution)/shard_map/all_gather | solution.py:120
  14.3 14.1 %copy-start.4 = (f32[128,512]{1,0:T(8,128)S(1)}, f32[128,512]{1,0:T(8,128)}, u32[]{:S(2)}) copy-start(f32[128,512]{1,0:T(8,128)} %param.22) | copy-start | bytes 786436
  14.3 14.1 %copy-start.5 = (f32[512,128]{1,0:T(8,128)S(1)}, f32[512,128]{1,0:T(8,128)}, u32[]{:S(2)}) copy-start(f32[512,128]{1,0:T(8,128)} %param.24) | copy-start | bytes 786436
  28.8 14.1 %copy-start.2 = (f32[4096,128]{1,0:T(8,128)S(1)}, f32[4096,128]{1,0:T(8,128)}, u32[]{:S(2)}) copy-start(f32[4096,128]{1,0:T(8,128)} %gather_fusion) | copy-start | bytes 6291460
  44.7 1.9 copy-start.12
  44.7 3.9 %copy-start.6 = (f32[128,512]{1,0:T(8,128)S(1)}, f32[128,512]{1,0:T(8,128)}, u32[]{:S(2)}) copy-start(f32[128,512]{1,0:T(8,128)} %param.25) | copy-start | bytes 786436
  48.6 20.1 %copy-start.10 = (f32[512]{0:T(512)S(1)}, f32[512]{0:T(512)}, u32[]{:S(2)}) copy-start(f32[512]{0:T(512)} %param.26) | copy-start | bytes 6148
  49.1 23.5 %copy-start.11 = (s32[64,16]{0,1:T(8,128)S(1)}, s32[64,16]{0,1:T(8,128)}, u32[]{:S(2)}) copy-start(s32[64,16]{0,1:T(8,128)} %param.37) | copy-start | bytes 12292
  67.3 7.9 %copy-start.3 = (f32[512,512]{1,0:T(8,128)S(1)}, f32[512,512]{1,0:T(8,128)}, u32[]{:S(2)}) copy-start(f32[512,512]{1,0:T(8,128)} %param.32) | copy-start | bytes 3145732
  161.3 13.7 %copy-start.1 = (f32[8192,256]{0,1:T(8,128)S(1)}, f32[8192,256]{0,1:T(8,128)}, u32[]{:S(2)}) copy-start(f32[8192,256]{0,1:T(8,128)} %all-gather.2.cloned.1.call-done) | copy-start | bytes 25165828
  175.0 5.0 %copy-start.7 = (f32[128,512]{1,0:T(8,128)S(1)}, f32[128,512]{1,0:T(8,128)}, u32[]{:S(2)}) copy-start(f32[128,512]{1,0:T(8,128)} %param.30) | copy-start | bytes 786436
  180.0 5.6 %copy-start.14 = (s32[48,2]{0,1:T(2,128)S(1)}, s32[48,2]{0,1:T(2,128)}, u32[]{:S(2)}) copy-start(s32[48,2]{0,1:T(2,128)} %param.40) | copy-start | bytes 1156
  180.0 5.6 %copy-start.9 = (s32[48,2,128]{2,1,0:T(2,128)S(1)}, s32[48,2,128]{2,1,0:T(2,128)}, u32[]{:S(2)}) copy-start(s32[48,2,128]{2,1,0:T(2,128)} %param.41) | copy-start | bytes 147460
  181.6 18.7 %all-to-all-start.1 = ((f32[4,128,512]{2,1,0:T(8,128)}), f32[4,128,512]{2,1,0:T(8,128)S(1)}, u32[]{:S(2)}, u32[]{:S(2)}) async-start(f32[4,128,512]{2,1,0:T(8,128)} %broadcast_in_dim.21), calls=%async_computation.1 | async-start | bytes 2097152 | tf_op jit(solution)/shard_map/all_to_all | solution.py:17
  185.6 124.3 %reduce-scatter.2.cloned.1.call-start = ((), (), s32[]{:S(2)}) async-start(), calls=%async_computation.4 | async-start | bytes 5242880 | tf_op jit(solution)/shard_map/reduce_scatter | solution.py:155
  185.7 16.6 %copy-start.13 = (f32[512]{0:T(512)S(1)}, f32[512]{0:T(512)}, u32[]{:S(2)}) copy-start(f32[512]{0:T(512)} %param.33) | copy-start | bytes 6148
  203.7 23.9 %collective-permute-start = (f32[128,128]{1,0:T(8,128)S(1)}, f32[128,128]{1,0:T(8,128)S(1)}, u32[]{:S(2)}, u32[]{:S(2)}) collective-permute-start(f32[128,128]{1,0:T(8,128)S(1)} %fusion.46), channel_id=1, source_target_pairs={{0,1},{1,2},{2,3},{3,4},{4,5},{5,6},{6,7},{7,8},{8,9},{9,10},{10,1... | collective-permute-start | bytes 196616 | tf_op jit(solution)/shard_map/ppermute | solution.py:34
  206.6 21.0 %collective-permute-start.1 = (f32[128,128]{1,0:T(8,128)S(1)}, f32[128,128]{1,0:T(8,128)S(1)}, u32[]{:S(2)}, u32[]{:S(2)}) collective-permute-start(f32[128,128]{1,0:T(8,128)S(1)} %fusion.46), channel_id=1, source_target_pairs={{1,0},{2,1},{3,2},{4,3},{5,4},{6,5},{7,6},{8,7},{9,8},{10,9},{11,1... | collective-permute-start | bytes 196616 | tf_op jit(solution)/shard_map/ppermute | solution.py:35
  254.7 3.3 %copy-start.8 = (f32[128,512]{1,0:T(8,128)S(1)}, f32[128,512]{1,0:T(8,128)}, u32[]{:S(2)}) copy-start(f32[128,512]{1,0:T(8,128)} %param.36) | copy-start | bytes 786436
Sparse Core Ops, SparseCore 0:
  72.8 88.5 all-gather.1
  263.0 46.8 reduce-scatter.1
where the time goes:
time: 321 us; the launch traced here: 319 us
  waiting for transfers between devices  142 us (44%)
  local copies, waits for them, and re-layouts  72.8 us (23%)
  matrix products  48.9 us (15%)
  blocking collectives  18.2 us (6%)
  other arithmetic  17.1 us (5%)
  between operations  13.8 us (4%)
  starting transfers between devices  6.86 us (2%)
    all_gather x1, waiting for transfers between devices, per_device(): key_piece = lax.all_gather(key_values, 'nodes', axis=0, tiled=True)  85.4 us
    reduce_scatter x1, waiting for transfers between devices, per_device(): lax.psum_scatter(product(dec_agg, dec_out_w), 'mp', scatter_dimension=1,...  47 us
    gather x2, local copies, waits for them, and re-layouts, edge_pass(): source_side[source] + target_side[target]  35 us
    gather x2, local copies, waits for them, and re-layouts, edge_pass(): target_side[target]  35 us
    dot_general x12, matrix products, product(): jnp.dot(matrix, weight, precision=FULL_PRECISION, preferred_element_type=...  24 us
    all_to_all x1, blocking collectives, copy_for_each(): lax.all_to_all(jnp.broadcast_to(shard[None], (devices, *shard.shape)), ax...  18.2 us
    dot_general x1, matrix products, per_device(): jnp.einsum('bqhd,khd->bhqk', query_blocks, near_keys, precision=FULL_PREC...  10.2 us
    all_to_all x1, waiting for transfers between devices, copy_for_each(): lax.all_to_all(jnp.broadcast_to(shard[None], (devices, *shard.shape)), ax...  9.34 us
  transfers between devices with their start and end apart: 5, of which 3 were waited for; matrix products, arithmetic and copies ran while one was open for 9% of the time, Pallas kernels for 0%

commit v1 on v0

v1 whole, which is shorter than its diff:
```python
import functools
import math

import jax
import jax.numpy as jnp
from jax import lax
from jax.experimental import pallas as pl
from jax.experimental.pallas import tpu as pltpu
from jax.sharding import PartitionSpec as P

HEAD_DIM = 128
BLOCK = 128
FULL = lax.Precision.HIGHEST
F32 = jnp.float32
BF16 = jnp.bfloat16


def product(matrix, weight):
    return jnp.dot(matrix, weight, precision=FULL, preferred_element_type=F32)


def layer_norm(inputs, scales):
    centre = jnp.mean(inputs, axis=-1, keepdims=True)
    shifted = inputs - centre
    spread = jnp.mean(shifted * shifted, axis=-1, keepdims=True)
    return shifted * lax.rsqrt(spread + 1e-05) * scales


def split(x):
    high = x.astype(BF16)
    low = (x - high.astype(F32)).astype(BF16)
    return high, low


def mm(a, b):
    return jnp.dot(a, b, preferred_element_type=F32)


def silu(v):
    return v * (1.0 / (1.0 + jnp.exp(-v)))


def as_column(row):
    return jnp.broadcast_to(row, (8, BLOCK)).T[:, 0:1]


def one_hot_rows(row):
    lane = lax.broadcasted_iota(jnp.int32, (BLOCK, BLOCK), 1)
    return jnp.where(as_column(row) == lane, 1.0, 0.0).astype(BF16)


def one_hot_cols(row):
    sub = lax.broadcasted_iota(jnp.int32, (BLOCK, BLOCK), 0)
    return jnp.where(row == sub, 1.0, 0.0).astype(BF16)


def encoder_kernel(
    tiles, grid_ref, wg_ref, mesh_ref, wm_ref, edges_ref, out_ref, wcat, gcat, mcat, acc
):
    step = pl.program_id(0)
    steps = pl.num_programs(0)
    rows, hid = grid_ref.shape[0], wg_ref.shape[1]
    blocks = gcat.shape[0] // BLOCK
    slots = edges_ref.shape[0]

    @pl.when(step == 0)
    def _():
        high, low = split(wg_ref[...])
        wcat[:, :hid] = high
        wcat[:, hid:] = low
        mesh_enc = product(mesh_ref[...], wm_ref[...])
        high, low = split(mesh_enc)
        mcat[:, :hid] = high
        mcat[:, hid:] = low
        acc[...] = jnp.zeros_like(acc)

    xh, xl = split(grid_ref[...])
    both = mm(xh, wcat[...]) + mm(xl, wcat[...])
    high, low = split(both[:, :hid] + both[:, hid:])
    here = pl.ds(pl.multiple_of(step * rows, rows), rows)
    gcat[here, :hid] = high
    gcat[here, hid:] = low

    @pl.when(step == steps - 1)
    def _():
        first = lax.axis_index("nodes") * blocks
        group = 4

        def body(i, carry):
            hots, messages = [], []
            for k in range(group):
                t = i * group + k
                tile = tiles[t, 0]
                live = tile >= 0
                block = jnp.where(live, tile - first, 0)
                ids = edges_ref[t]
                source = one_hot_rows(ids[0:1])
                target = one_hot_rows(ids[1:2])
                picked = jnp.concatenate([source, target], axis=1)
                block_rows = gcat[pl.ds(pl.multiple_of(block * BLOCK, BLOCK), BLOCK), :]
                table = jnp.concatenate([block_rows, mcat[...]], axis=0)
                pre = mm(picked, table)
                mh, ml = split(silu(pre[:, :hid] + pre[:, hid:]))
                messages.append(jnp.concatenate([mh, ml], axis=1))
                hots.append(one_hot_cols(jnp.where(live, ids[1:2], -1)))
            acc[...] += mm(jnp.concatenate(hots, axis=1), jnp.concatenate(messages, axis=0))
            return carry

        lax.fori_loop(0, slots // group, body, 0)
        out_ref[...] = acc[:, :hid] + acc[:, hid:]


def encoder(grid_latent, mesh_latent, enc_grid_w, enc_mesh_w, enc_tiles, enc_edges):
    rows, width = grid_latent.shape
    hid = enc_grid_w.shape[1]
    nodes = mesh_latent.shape[0]
    chunk = 512
    return pl.pallas_call(
        encoder_kernel,
        grid_spec=pltpu.PrefetchScalarGridSpec(
            num_scalar_prefetch=1,
            grid=(rows // chunk,),
            in_specs=[
                pl.BlockSpec((chunk, width), lambda i, t: (i, 0)),
                pl.BlockSpec((width, hid), lambda i, t: (0, 0)),
                pl.BlockSpec((nodes, width), lambda i, t: (0, 0)),
                pl.BlockSpec((width, hid), lambda i, t: (0, 0)),
                pl.BlockSpec(enc_edges.shape, lambda i, t: (0, 0, 0)),
            ],
            out_specs=pl.BlockSpec((nodes, hid), lambda i, t: (0, 0)),
            scratch_shapes=[
                pltpu.VMEM((width, 2 * hid), BF16),
                pltpu.VMEM((rows, 2 * hid), BF16),
                pltpu.VMEM((nodes, 2 * hid), BF16),
                pltpu.VMEM((nodes, 2 * hid), F32),
            ],
        ),
        out_shape=jax.ShapeDtypeStruct((nodes, hid), F32),
        compiler_params=pltpu.CompilerParams(vmem_limit_bytes=40 << 20),
        cost_estimate=pl.CostEstimate(
            flops=2 * 6 * rows * width * hid, bytes_accessed=6 << 20, transcendentals=1 << 20
        ),
        name="encoder",
    )(enc_tiles, grid_latent, enc_grid_w, mesh_latent, enc_mesh_w, enc_edges)


def decoder_kernel(
    tiles, grid_ref, wg_ref, mesh_ref, wo_ref, edges_ref, out_ref, gcat, mcat, wcat, agg
):
    rows, width = grid_ref.shape
    hid = wg_ref.shape[1]
    blocks = rows // BLOCK
    mp = lax.axis_size("mp")
    node = lax.axis_index("nodes")
    nodes = lax.axis_size("nodes")
    first = (node * mp + lax.axis_index("mp")) * blocks

    wh, wl = split(wg_ref[...])
    wcat[:, :hid] = wh
    wcat[:, hid:] = wl
    for b in range(blocks):
        here = slice(b * BLOCK, (b + 1) * BLOCK)
        xh, xl = split(grid_ref[here, :])
        high, low = split(mm(xh, wcat[:, :hid]) + mm(xh, wcat[:, hid:]) + mm(xl, wcat[:, :hid]))
        gcat[here, :hid] = high
        gcat[here, hid:] = low
    high, low = split(mesh_ref[...])
    mcat[:, :hid] = high
    mcat[:, hid:] = low
    agg[...] = jnp.zeros_like(agg)

    def body(t, carry):
        block = tiles[t, 1] - first

        @pl.when(jnp.logical_and(block >= 0, block < blocks))
        def _():
            beside = lax.rem(tiles[t, 0] - (node - 1) + nodes, nodes)
            ids = edges_ref[t]
            source = one_hot_rows(ids[0:1])
            target = one_hot_rows(ids[1:2])
            picked = jnp.concatenate([source, target], axis=1)
            here = pl.ds(pl.multiple_of(block * BLOCK, BLOCK), BLOCK)
            there = pl.ds(pl.multiple_of(beside * BLOCK, BLOCK), BLOCK)
            table = jnp.concatenate([mcat[there, :], gcat[here, :]], axis=0)
            pre = mm(picked, table)
            mh, ml = split(silu(pre[:, :hid] + pre[:, hid:]))
            hot = one_hot_cols(ids[1:2])
            agg[here, :] += mm(hot, mh) + mm(hot, ml)

        return carry

    lax.fori_loop(0, edges_ref.shape[0], body, 0)
    wh, wl = split(wo_ref[...])
    for b in range(blocks):
        here = slice(b * BLOCK, (b + 1) * BLOCK)
        ah, al = split(agg[here, :])
        out_ref[here, :] = grid_ref[here, :] + (mm(ah, wh) + mm(ah, wl) + mm(al, wh))


def decoder(grid_latent, dec_grid_w, mesh_beside, dec_out_w, dec_tiles, dec_edges):
    rows, width = grid_latent.shape
    hid = dec_grid_w.shape[1]
    vmem = pl.BlockSpec(memory_space=pltpu.VMEM)
    share = rows // lax.axis_size("mp")
    me = lax.axis_index("mp")
    mine = lax.dynamic_slice_in_dim(grid_latent, me * share, share, 0)
    return pl.pallas_call(
        decoder_kernel,
        in_specs=[pl.BlockSpec(memory_space=pltpu.SMEM)] + [vmem] * 5,
        out_specs=vmem,
        out_shape=jax.ShapeDtypeStruct((share, width), F32),
        scratch_shapes=[
            pltpu.VMEM((share, 2 * hid), BF16),
            pltpu.VMEM((mesh_beside.shape[0], 2 * hid), BF16),
            pltpu.VMEM((width, 2 * hid), BF16),
            pltpu.VMEM((share, hid), F32),
        ],
        compiler_params=pltpu.CompilerParams(vmem_limit_bytes=40 << 20),
        cost_estimate=pl.CostEstimate(
            flops=2 * 6 * share * width * hid, bytes_accessed=6 << 20, transcendentals=1 << 20
        ),
        name="decoder",
    )(dec_tiles, mine, dec_grid_w, mesh_beside, dec_out_w, dec_edges)


def attention_kernel(listed, query_ref, near_ref, out_ref, scores, values):
    step = pl.program_id(0)
    near = near_ref[0]
    here = pl.ds(pl.multiple_of(step * BLOCK, BLOCK), BLOCK)
    scores[:, here] = lax.dot_general(
        query_ref[...],
        near[:, :HEAD_DIM],
        (((1,), (1,)), ((), ())),
        precision=FULL,
        preferred_element_type=F32,
    ) * (1.0 / math.sqrt(HEAD_DIM))
    values[here, :] = near[:, HEAD_DIM:]

    @pl.when(step == pl.num_programs(0) - 1)
    def _():
        logits = scores[...]
        weights = jnp.exp(logits - jnp.max(logits, axis=-1, keepdims=True))
        total = jnp.sum(weights, axis=-1, keepdims=True)
        out_ref[...] = product(weights, values[...]) / total


def attention(queries, everything, neighbor_blocks):
    listed = neighbor_blocks.shape[1]
    rows = queries.shape[0]
    return pl.pallas_call(
        attention_kernel,
        grid_spec=pltpu.PrefetchScalarGridSpec(
            num_scalar_prefetch=1,
            grid=(listed,),
            in_specs=[
                pl.BlockSpec((rows, HEAD_DIM), lambda i, t: (0, 0)),
                pl.BlockSpec(
                    (1, BLOCK, 2 * HEAD_DIM), lambda i, t: (t[lax.axis_index("nodes"), i], 0, 0)
                ),
            ],
            out_specs=pl.BlockSpec((rows, HEAD_DIM), lambda i, t: (0, 0)),
            scratch_shapes=[
                pltpu.VMEM((rows, listed * BLOCK), F32),
                pltpu.VMEM((listed * BLOCK, HEAD_DIM), F32),
            ],
        ),
        out_shape=jax.ShapeDtypeStruct((rows, HEAD_DIM), F32),
        compiler_params=pltpu.CompilerParams(vmem_limit_bytes=24 << 20),
        name="attention",
    )(neighbor_blocks, queries, everything)


def per_device(
    grid_latent,
    mesh_latent,
    enc_grid_w,
    enc_mesh_w,
    enc_out_w,
    block_gain,
    query_w,
    key_w,
    value_w,
    out_w,
    up_w,
    down_w,
    dec_gain,
    dec_grid_w,
    dec_mesh_w,
    dec_out_w,
    neighbor_blocks,
    enc_tiles,
    enc_edges,
    dec_tiles,
    dec_edges,
):
    me_node = lax.axis_index("nodes")
    count = lax.axis_size("nodes")
    node_rows = mesh_latent.shape[0]
    outs = jnp.concatenate([enc_out_w, out_w, dec_out_w], axis=1)
    outs = lax.all_gather(outs, "mp", axis=0, tiled=True)
    enc_out_all, out_all, dec_out_all = jnp.split(outs, 3, axis=1)
    dec_grid_all = lax.all_gather(dec_grid_w.T, "mp", axis=0, tiled=True).T
    dec_mesh_all = lax.all_gather(dec_mesh_w.T, "mp", axis=0, tiled=True).T

    enc_agg = encoder(grid_latent, mesh_latent, enc_grid_w, enc_mesh_w, enc_tiles, enc_edges)
    enc_agg = lax.all_gather(enc_agg, "mp", axis=1, tiled=True)
    mesh_one = mesh_latent + product(enc_agg, enc_out_all)
    normed = layer_norm(mesh_one, block_gain)
    queries = product(normed, query_w)
    key_values = jnp.concatenate([product(normed, key_w), product(normed, value_w)], axis=1)
    everything = lax.all_gather(key_values, "nodes", axis=0, tiled=False)
    hidden = jax.nn.silu(product(normed, up_w))
    mlp = lax.psum(product(hidden, down_w), "mp")
    attended = attention(queries, everything, neighbor_blocks)
    attended = lax.all_gather(attended, "mp", axis=1, tiled=True)
    mesh_two = mesh_one + mlp + product(attended, out_all)
    mesh_dec = product(layer_norm(mesh_two, dec_gain), dec_mesh_all)
    up = [(i, (i + 1) % count) for i in range(count)]
    down = [(j, i) for i, j in up]
    before = lax.ppermute(mesh_dec, "nodes", up)
    after = lax.ppermute(mesh_dec, "nodes", down)
    beside = jnp.concatenate([before, mesh_dec, after], axis=0)
    rows_out = decoder(grid_latent, dec_grid_all, beside, dec_out_all, dec_tiles, dec_edges)
    return lax.all_to_all(rows_out, "mp", split_axis=1, concat_axis=0, tiled=True)


def solution(mesh):
    in_specs = (
        P("nodes", None),
        P("nodes", None),
        P(None, "mp"),
        P(None, "mp"),
        P("mp", None),
        P(),
        P(None, "mp"),
        P(None, "mp"),
        P(None, "mp"),
        P("mp", None),
        P(None, "mp"),
        P("mp", None),
        P(),
        P(None, "mp"),
        P(None, "mp"),
        P("mp", None),
        P(),
        P("nodes", None),
        P("nodes", None, None),
        P("nodes", None),
        P("nodes", None, None),
    )
    out_specs = P("nodes", "mp")
    return jax.shard_map(
        per_device, mesh=mesh, in_specs=in_specs, out_specs=out_specs, check_vma=False
    )
```

time: 321 us -> 303 us (0.944)
  local copies, waits for them, and re-layouts: 72.8 us -> 25.1 us
  matrix products: 48.9 us -> 9.96 us
  waiting for transfers between devices: 142 us -> 172 us
  Pallas kernels: 0 us -> 29.2 us
  blocking collectives: 18.2 us -> 42.2 us
  other arithmetic: 17.1 us -> 5.12 us
  starting transfers between devices: 6.86 us -> 2.86 us
    gather x4 -> x0, local copies, waits for them, and re-layouts: 70 us -> none  [the longest x2 35 us: edge_pass(): source_side[source] + target_side[target]]
    all_gather x1 -> x4, waiting for transfers between devices: 85.4 us -> 151 us  [the longest x1 82.7 us: per_device(): everything = lax.all_gather(key_values, 'nodes', axis=0, tiled=False)]
    reduce_scatter x1 -> x0, waiting for transfers between devices: 47 us -> none  [per_device(): lax.psum_scatter(product(dec_agg, dec_out_w), 'mp', scatter_dimension=1,...]
    dot_general x18 -> x8, matrix products: 48.9 us -> 9.96 us  [product(): return jnp.dot(matrix, weight, precision=FULL, preferred_element_type=F32)]
    pallas_call x0 -> x3, Pallas kernels: none -> 29.2 us  [the longest x1 13.4 us: decoder(): pl.pallas_call(decoder_kernel, in_specs=[pl.BlockSpec(memory_space=pltpu....]
    all_gather x0 -> x2, blocking collectives: none -> 22.7 us  [the longest x1 12.3 us: per_device(): enc_agg = lax.all_gather(enc_agg, 'mp', axis=1, tiled=True)]
    psum x0 -> x1, waiting for transfers between devices: none -> 16.8 us  [per_device(): mlp = lax.psum(product(hidden, down_w), 'mp')]
    unnamed x30 -> x42, local copies, waits for them, and re-layouts: 0.09 us -> 13.5 us
  transfers between devices with their start and end apart: 5 -> 7, of which waited for: 3 -> 7; matrix products, arithmetic and copies ran while one was open for 9% -> 7% of each run, Pallas kernels for 0% -> 5%
where the time goes in v1:
time: 303 us; the launch traced here: 300 us
  waiting for transfers between devices  172 us (57%)
  blocking collectives  42.2 us (14%)
  Pallas kernels  29.2 us (10%)
  local copies, waits for them, and re-layouts  25.1 us (8%)
  between operations  13.4 us (4%)
  matrix products  9.96 us (3%)
  other arithmetic  5.12 us (2%)
    all_gather x1, waiting for transfers between devices, per_device(): everything = lax.all_gather(key_values, 'nodes', axis=0, tiled=False)  82.7 us
    all_gather x1, waiting for transfers between devices, per_device(): dec_mesh_all = lax.all_gather(dec_mesh_w.T, 'mp', axis=0, tiled=True).T  29.7 us
    all_gather x1, waiting for transfers between devices, per_device(): outs = lax.all_gather(outs, 'mp', axis=0, tiled=True)  19.6 us
    all_to_all x1, blocking collectives, per_device(): lax.all_to_all(rows_out, 'mp', split_axis=1, concat_axis=0, tiled=True)  19.5 us
    all_gather x1, waiting for transfers between devices, per_device(): dec_grid_all = lax.all_gather(dec_grid_w.T, 'mp', axis=0, tiled=True).T  18.7 us
    psum x1, waiting for transfers between devices, per_device(): mlp = lax.psum(product(hidden, down_w), 'mp')  16.8 us
    unnamed x42, local copies, waits for them, and re-layouts  13.5 us
    pallas_call x1, Pallas kernels, decoder(): pl.pallas_call(decoder_kernel, in_specs=[pl.BlockSpec(memory_space=pltpu....  13.4 us
  transfers between devices with their start and end apart: 7, of which 7 were waited for; matrix products, arithmetic and copies ran while one was open for 7% of the time, Pallas kernels for 5%

profile of v1, /device:TPU:3, one launch (start us, length us, event | category | flops | bytes accessed | tf_op | source)
XLA Modules:
  0.0 299.8 jit_solution(9005122784196582178)
XLA Ops:
  6.5 2.1 pad_maximum_fusion
  9.5 2.2 copy-done.3
  15.3 9.2 %encoder.1 = f32[128,128]{1,0:T(8,128)S(1)} custom-call(s32[32,2]{1,0:T(8,128)S(1)} %copy.27.tiles, f32[2048,512]{1,0:T(8,128)S(1)} %copy-done.3, f32[512,128]{1,0:T(8,128)S(1)} %copy-done.7, f32[128,512]{1,0:T(8,128)S(1)} %copy-done.4, f32[512,128]{1,0:T(8,128)S(1)} %copy-done.8, s32[32,2,128]{2,1,0:T(2,128)S(1)} %copy-done.10), custom_call_target="tpu_custom_call" | custom-call | flops 1610612736 | bytes 6291456 | tf_op jit(solution)/shard_map/encoder/pallas_call | solution.py:118
  24.5 12.3 %all_gather.22 = f32[128,512]{1,0:T(8,128)S(1)} all-gather(f32[128,128]{1,0:T(8,128)S(1)} %encoder.1), channel_id=1, replica_groups=mesh['mp'=4,'nodes'=64] {'mp'}, dimensions={1}, use_global_device_ids=true | all-gather | bytes 327680 | tf_op jit(solution)/shard_map/all_gather | solution.py:306
  36.8 19.6 %all-gather.8.cloned.1.call-done = f32[512,1536]{1,0:T(8,128)} async-done(((f32[128,1536]{1,0:T(8,128)}), f32[512,1536]{1,0:T(8,128)}) %all-gather.8.cloned.1.call-update) | async-done | bytes 3145744 | tf_op jit(solution)/shard_map/all_gather | solution.py:300
  56.4 2.0 fusion.21
  61.5 1.5 fusion.5
  64.6 82.7 %all-gather.12.cloned.1.call-done = f32[8192,256]{0,1:T(8,128)} async-done(((f32[128,256]{0,1:T(8,128)}), f32[8192,256]{0,1:T(8,128)}) %all-gather.12.cloned.1.call-update) | async-done | bytes 8388624 | tf_op jit(solution)/shard_map/all_gather | solution.py:311
  147.4 9.0 %copy.28 = f32[8192,256]{1,0:T(8,128)} copy(f32[8192,256]{0,1:T(8,128)} %all-gather.12.cloned.1.call-done) | data formatting | bytes 16777216 | tf_op jit(solution)/shard_map/all_gather | solution.py:311
  156.4 3.4 %copy-done.1 = f32[8192,256]{1,0:T(8,128)S(1)} copy-done((f32[8192,256]{1,0:T(8,128)S(1)}, f32[8192,256]{1,0:T(8,128)}, u32[]{:S(2)}) %copy-start.1) | copy-done | bytes 8388632
  159.8 6.7 %attention.1 = f32[128,128]{1,0:T(8,128)S(1)} custom-call(s32[64,16]{1,0:T(8,128)S(1)} %copy.29.listed, f32[128,128]{1,0:T(8,128)S(1)} %fusion.19.query_ref, f32[64,128,256]{2,1,0:T(8,128)S(1)} %bitcast.20), custom_call_target="tpu_custom_call" | custom-call | tf_op jit(solution)/shard_map/attention/pallas_call | solution.py:250
  166.4 10.3 %all_gather.26 = f32[128,512]{1,0:T(8,128)S(1)} all-gather(f32[128,128]{1,0:T(8,128)S(1)} %attention.1), channel_id=1, replica_groups=mesh['mp'=4,'nodes'=64] {'mp'}, dimensions={1}, use_global_device_ids=true | all-gather | bytes 327680 | tf_op jit(solution)/shard_map/all_gather | solution.py:315
  176.8 16.8 %all-reduce.2.cloned.1.call-done = f32[128,512]{1,0:T(8,128)} async-done(((f32[128,512]{1,0:T(8,128)}), f32[128,512]{1,0:T(8,128)}) %all-reduce.2.cloned.1.call-update) | async-done | bytes 262160 | tf_op jit(solution)/shard_map/psum | solution.py:313
  193.6 2.1 fusion.22
  195.8 29.7 %all-gather.10.cloned.1.call-done = f32[512,512]{0,1:T(8,128)} async-done(((f32[128,512]{0,1:T(8,128)}), f32[512,512]{0,1:T(8,128)}) %all-gather.10.cloned.1.call-update) | async-done | bytes 1048592 | tf_op jit(solution)/shard_map/all_gather | solution.py:303
  225.6 2.0 fusion.2
  227.6 2.7 collective-permute-start
  230.4 1.3 constant_dynamic-slice_fusion.grid_ref
  231.7 1.3 split.14.wo_ref
  233.6 2.6 collective-permute-done.1
  236.2 2.0 pad_maximum_fusion.1.mesh_ref
  238.1 18.7 %all-gather.6.cloned.1.call-done = f32[512,512]{0,1:T(8,128)} async-done(((f32[128,512]{0,1:T(8,128)}), f32[512,512]{0,1:T(8,128)}) %all-gather.6.cloned.1.call-update) | async-done | bytes 1048592 | tf_op jit(solution)/shard_map/all_gather | solution.py:302
  259.2 13.4 %decoder.1 = f32[512,512]{1,0:T(8,128)S(1)} custom-call(s32[48,2]{1,0:T(8,128)S(1)} %copy.30.tiles, f32[512,512]{1,0:T(8,128)S(1)} %constant_dynamic-slice_fusion.grid_ref, f32[512,512]{1,0:T(8,128)S(1)} %bitcast.21, f32[384,512]{1,0:T(8,128)S(1)} %copy-done.2, f32[512,512]{1,0:T(8,128)S(1)} %split.14.wo_ref, s32[48,2,128]{2,1,0:T(2,128)S(1)} %copy-done.9), custom_call_target="tpu_custom_call" | custom-call | flops 1610612736 | bytes 6291456 | tf_op jit(solution)/shard_map/decoder/pallas_call | solution.py:207
  272.7 19.5 %all_to_all.19 = f32[512,4,128]{2,0,1:T(8,128)S(1)} all-to-all(f32[512,4,128]{2,0,1:T(8,128)S(1)} %copy_bitcast_fusion), channel_id=1, replica_groups=mesh['mp'=4,'nodes'=64] {'mp'}, dimensions={1} | all-to-all | bytes 2097152 | tf_op jit(solution)/shard_map/all_to_all | solution.py:324
  (64 shorter events, 13.4 us)
Async XLA Ops:
  6.5 54.2 %copy-start = (f32[512,512]{1,0:T(8,128)S(1)}, f32[512,512]{1,0:T(8,128)}, u32[]{:S(2)}) copy-start(f32[512,512]{1,0:T(8,128)} %param.31) | copy-start | bytes 3145732
  6.5 49.8 %all-gather.8.cloned.1.call-start = ((), (), s32[]{:S(2)}) async-start(), calls=%async_computation.2 | async-start | bytes 3932160 | tf_op jit(solution)/shard_map/all_gather | solution.py:300
  8.7 138.7 %all-gather.12.cloned.1.call-start = ((), (), s32[]{:S(2)}) async-start(), calls=%async_computation.5 | async-start | bytes 8519680 | tf_op jit(solution)/shard_map/all_gather | solution.py:311
  9.5 2.2 copy-start.3
  11.7 0.9 copy-start.4
  12.7 0.9 copy-start.7
  15.3 41.1 %copy-start.5 = (f32[128,512]{1,0:T(8,128)S(1)}, f32[128,512]{1,0:T(8,128)}, u32[]{:S(2)}) copy-start(f32[128,512]{1,0:T(8,128)} %mesh_ref.1) | copy-start | bytes 786436
  15.3 43.3 %copy-start.12 = (f32[512,128]{1,0:T(8,128)S(1)}, f32[512,128]{1,0:T(8,128)}, u32[]{:S(2)}) copy-start(f32[512,128]{1,0:T(8,128)} %param.28) | copy-start | bytes 786436
  15.3 43.3 %copy-start.15 = (f32[512]{0:T(512)S(1)}, f32[512]{0:T(512)}, u32[]{:S(2)}) copy-start(f32[512]{0:T(512)} %param.26) | copy-start | bytes 6148
  15.3 44.0 %copy-start.13 = (f32[512,128]{1,0:T(8,128)S(1)}, f32[512,128]{1,0:T(8,128)}, u32[]{:S(2)}) copy-start(f32[512,128]{1,0:T(8,128)} %param.29) | copy-start | bytes 786436
  24.5 37.0 %copy-start.11 = (f32[512,512]{1,0:T(8,128)S(1)}, f32[512,512]{1,0:T(8,128)}, u32[]{:S(2)}) copy-start(f32[512,512]{1,0:T(8,128)} %param.32) | copy-start | bytes 3145732
  58.4 5.7 %copy-start.16 = (s32[64,16]{0,1:T(8,128)S(1)}, s32[64,16]{0,1:T(8,128)}, u32[]{:S(2)}) copy-start(s32[64,16]{0,1:T(8,128)} %param.37) | copy-start | bytes 12292
  58.4 5.8 %copy-start.14 = (f32[512,128]{1,0:T(8,128)S(1)}, f32[512,128]{1,0:T(8,128)}, u32[]{:S(2)}) copy-start(f32[512,128]{1,0:T(8,128)} %param.27) | copy-start | bytes 786436
  60.6 132.9 %all-reduce.2.cloned.1.call-start = ((), (), s32[]{:S(2)}) async-start(), calls=%async_computation.3 | async-start | bytes 524288 | tf_op jit(solution)/shard_map/psum | solution.py:313
  62.9 162.6 %all-gather.10.cloned.1.call-start = ((), (), s32[]{:S(2)}) async-start(), calls=%async_computation.4 | async-start | bytes 1310720 | tf_op jit(solution)/shard_map/all_gather | solution.py:303
  63.5 193.3 %all-gather.6.cloned.1.call-start = ((), (), s32[]{:S(2)}) async-start(), calls=%async_computation.1 | async-start | bytes 1310720 | tf_op jit(solution)/shard_map/all_gather | solution.py:302
  156.4 3.4 %copy-start.1 = (f32[8192,256]{1,0:T(8,128)S(1)}, f32[8192,256]{1,0:T(8,128)}, u32[]{:S(2)}) copy-start(f32[8192,256]{1,0:T(8,128)} %copy.28) | copy-start | bytes 25165828
  159.8 65.8 %copy-start.17 = (f32[512]{0:T(512)S(1)}, f32[512]{0:T(512)}, u32[]{:S(2)}) copy-start(f32[512]{0:T(512)} %param.33) | copy-start | bytes 6148
  166.4 63.8 %copy-start.18 = (s32[48,2]{0,1:T(2,128)S(1)}, s32[48,2]{0,1:T(2,128)}, u32[]{:S(2)}) copy-start(s32[48,2]{0,1:T(2,128)} %param.40) | copy-start | bytes 1156
  227.6 29.3 %copy-start.9 = (s32[48,2,128]{2,1,0:T(2,128)S(1)}, s32[48,2,128]{2,1,0:T(2,128)}, u32[]{:S(2)}) copy-start(s32[48,2,128]{2,1,0:T(2,128)} %edges_ref.3) | copy-start | bytes 147460
  227.6 6.0 %collective-permute-start = (f32[128,512]{1,0:T(8,128)S(1)}, f32[128,512]{1,0:T(8,128)}, u32[]{:S(2)}, u32[]{:S(2)}) collective-permute-start(f32[128,512]{1,0:T(8,128)S(1)} %fusion.2), channel_id=1, source_target_pairs={{0,1},{1,2},{2,3},{3,4},{4,5},{5,6},{6,7},{7,8},{8,9},{9,10},{10,1... | collective-permute-start | bytes 786440 | tf_op jit(solution)/shard_map/ppermute | solution.py:320
  230.3 5.9 %collective-permute-start.1 = (f32[128,512]{1,0:T(8,128)S(1)}, f32[128,512]{1,0:T(8,128)}, u32[]{:S(2)}, u32[]{:S(2)}) collective-permute-start(f32[128,512]{1,0:T(8,128)S(1)} %fusion.2), channel_id=1, source_target_pairs={{1,0},{2,1},{3,2},{4,3},{5,4},{6,5},{7,6},{8,7},{9,8},{10,9},{11,1... | collective-permute-start | bytes 786440 | tf_op jit(solution)/shard_map/ppermute | solution.py:321
  256.8 1.1 copy-start.2
  258.0 1.2 copy-start.6
  (2 other events, 1.7 us)
Sparse Core Ops, SparseCore 0:
  9.2 47.1 all-gather.7
  60.8 86.5 all-gather.11
  149.7 43.8 all-reduce.1
  195.4 30.1 all-gather.9
  227.4 29.4 all-gather.5

commit v2 on v1

v2 whole, which is shorter than its diff:
```python
import math

import jax
import jax.numpy as jnp
from jax import lax
from jax.experimental import pallas as pl
from jax.experimental.pallas import tpu as pltpu
from jax.sharding import PartitionSpec as P

HEAD_DIM = 128
BLOCK = 128
FULL = lax.Precision.HIGHEST
F32 = jnp.float32
BF16 = jnp.bfloat16


def product(matrix, weight):
    return jnp.dot(matrix, weight, precision=FULL, preferred_element_type=F32)


def split(x):
    high = x.astype(BF16)
    low = (x - high.astype(F32)).astype(BF16)
    return high, low


def mm(a, b):
    return jnp.dot(a, b, preferred_element_type=F32)


def silu(v):
    return v * (1.0 / (1.0 + jnp.exp(-v)))


def as_column(row):
    return jnp.broadcast_to(row, (8, BLOCK)).T[:, 0:1]


def one_hot_rows(row):
    lane = lax.broadcasted_iota(jnp.int32, (BLOCK, BLOCK), 1)
    return jnp.where(as_column(row) == lane, 1.0, 0.0).astype(BF16)


def one_hot_cols(row):
    sub = lax.broadcasted_iota(jnp.int32, (BLOCK, BLOCK), 0)
    return jnp.where(row == sub, 1.0, 0.0).astype(BF16)


MESH = pl.DeviceIdType.MESH
Z, X, MP = 8, 4, 4
CHIPS = Z * X
CHUNKS = ((0, 40), (40, 40), (80, 24), (104, 24))


def spans(chunk):
    plus = chunk % 2 == 0
    zs = (-3, 4) if plus else (-4, 3)
    xs = (-1, 2) if plus else (-2, 1)
    return zs, xs


def onward(chunk, dz, dx):
    zs, xs = spans(chunk)
    steps = []

    def along_z(start):
        if dz >= 0 and dz + 1 <= zs[1] and (start or dz > 0):
            steps.append((1, 0))
        if dz <= 0 and dz - 1 >= zs[0] and (start or dz < 0):
            steps.append((-1, 0))

    def along_x(start):
        if dx >= 0 and dx + 1 <= xs[1] and (start or dx > 0):
            steps.append((0, 1))
        if dx <= 0 and dx - 1 >= xs[0] and (start or dx < 0):
            steps.append((0, -1))

    if chunk < 2:
        if dx == 0:
            along_z(dz == 0)
            along_x(True)
        else:
            along_x(False)
    else:
        if dz == 0:
            along_x(dx == 0)
            along_z(True)
        else:
            along_z(False)
    return steps


def arrivals():
    events = []
    for chunk in range(4):
        zs, xs = spans(chunk)
        for dz in range(zs[0], zs[1] + 1):
            for dx in range(xs[0], xs[1] + 1):
                if (dz, dx) != (0, 0):
                    slot = (dz - zs[0]) * X + dx - xs[0]
                    events.append((abs(dz) + abs(dx), abs(dz), chunk, dz, dx, slot))
    return sorted(events)


def slot_of(chunk, dz, dx):
    zs, xs = spans(chunk)
    return (dz - zs[0]) * X + dx - xs[0]


def norm_rows(x, gain):
    centre = jnp.mean(x, axis=-1, keepdims=True)
    shifted = x - centre
    spread = jnp.mean(shifted * shifted, axis=-1, keepdims=True)
    return shifted * lax.rsqrt(spread + 1e-05) * gain


def mm3(ah, al, bh, bl):
    return mm(ah, bh) + mm(ah, bl) + mm(al, bh)


def mesh_kernel(
    tiles,
    lists,
    grid_ref,
    mesh_ref,
    enc_grid_w,
    enc_mesh_w,
    enc_edges,
    enc_out_w,
    gain_one,
    query_w,
    key_w,
    value_w,
    out_w,
    up_w,
    down_w,
    gain_two,
    dec_grid_w,
    dec_mesh_w,
    dec_out_w,
    beside,
    dec_grid_all,
    dec_out_all,
    wcat,
    gcat,
    mcat,
    acc,
    agg_all,
    enc_out_all,
    out_all,
    dec_mesh_all,
    kv,
    partial,
    parts,
    summed,
    att_all,
    scores,
    y_send,
    y_recv,
    c_send,
    c_recv,
    link_send,
    link_recv,
    core_send,
    core_recv,
    side_send,
    side_recv,
):
    me = lax.axis_index("mp")
    node = lax.axis_index("nodes")
    nodes = Z * X * 2
    core = lax.rem(node, 2)
    chip = node // 2
    z, x = chip // X, lax.rem(chip, X)
    z_at = {d: lax.rem(z + d + 2 * Z, Z) for d in range(-4, 5)}
    x_at = {d: lax.rem(x + d + 2 * X, X) for d in range(-2, 3)}
    sibling = node + 1 - 2 * core
    y_at = [lax.rem(me + k, MP) for k in range(MP)]
    y_from = [lax.rem(me + MP - k, MP) for k in range(MP)]
    after, before = lax.rem(node + 1, nodes), lax.rem(node + nodes - 1, nodes)
    beyond = jnp.where(core == 0, before, after)

    def chip_node(dz, dx):
        return (z_at[dz] * X + x_at[dx]) * 2 + core

    barrier = pltpu.get_barrier_semaphore()
    for dz, dx in ((1, 0), (-1, 0), (0, 1), (0, -1)):
        pl.semaphore_signal(
            barrier, inc=1, device_id={"nodes": chip_node(dz, dx)}, device_id_type=MESH
        )
    pl.semaphore_signal(barrier, inc=1, device_id={"nodes": sibling}, device_id_type=MESH)
    pl.semaphore_signal(barrier, inc=1, device_id={"nodes": beyond}, device_id_type=MESH)
    for k in range(1, MP):
        pl.semaphore_signal(barrier, inc=1, device_id={"mp": y_at[k]}, device_id_type=MESH)
    pl.semaphore_wait(barrier, 9)

    def y_copy(item, k, src, dst):
        return pltpu.make_async_remote_copy(
            src_ref=src,
            dst_ref=dst,
            send_sem=y_send.at[item, k - 1],
            recv_sem=y_recv.at[item, k - 1],
            device_id={"mp": y_at[k]},
            device_id_type=MESH,
        )

    def c_copy(item, k, ref):
        return pltpu.make_async_remote_copy(
            src_ref=ref,
            dst_ref=ref,
            send_sem=c_send.at[item, k - 1],
            recv_sem=c_recv.at[item, k - 1],
            device_id={"nodes": sibling},
            device_id_type=MESH,
        )

    weights = {
        0: (enc_out_w, enc_out_all),
        1: (dec_grid_w, dec_grid_all),
        2: (out_w, out_all),
        3: (dec_mesh_w, dec_mesh_all),
        4: (dec_out_w, dec_out_all),
    }

    def halves(item):
        half = weights[item][0].shape[0] // 2
        return pl.ds(pl.multiple_of(core * half, half), half), pl.ds(
            pl.multiple_of((1 - core) * half, half), half
        )

    def weight_start(item):
        own, whole = weights[item]
        mine, _ = halves(item)
        for k in range(1, MP):
            y_copy(item, k, own.at[mine], whole.at[me, mine]).start()
        whole[me] = own[...]

    def weight_pass_on(item):
        own, whole = weights[item]
        mine, _ = halves(item)
        for k in range(1, MP):
            y_copy(item, k, own.at[mine], whole.at[y_from[k], mine]).wait_recv()
            c_copy(item, k, whole.at[y_from[k], mine]).start()

    def weight_finish(item):
        own, whole = weights[item]
        mine, other = halves(item)
        for k in range(1, MP):
            c_copy(item, k, whole.at[y_from[k], other]).wait_recv()
        for k in range(1, MP):
            y_copy(item, k, own.at[mine], whole.at[me, mine]).wait_send()
            c_copy(item, k, whole.at[y_from[k], mine]).wait_send()

    weight_start(0)
    weight_start(1)

    rows, hid = grid_ref.shape[0], enc_grid_w.shape[1]
    blocks = rows // BLOCK
    slots = enc_edges.shape[0]
    high, low = split(enc_grid_w[...])
    wcat[:, :hid] = high
    wcat[:, hid:] = low
    high, low = split(product(mesh_ref[...], enc_mesh_w[...]))
    mcat[:, :hid] = high
    mcat[:, hid:] = low
    acc[...] = jnp.zeros_like(acc)
    chunk_rows = 256

    def project(i, carry):
        here = pl.ds(pl.multiple_of(i * chunk_rows, chunk_rows), chunk_rows)
        xh, xl = split(grid_ref[here, :])
        both = mm(xh, wcat[...]) + mm(xl, wcat[...])
        high, low = split(both[:, :hid] + both[:, hid:])
        for j in range(chunk_rows // BLOCK):
            part = slice(j * BLOCK, (j + 1) * BLOCK)
            gcat[i * (chunk_rows // BLOCK) + j, :, :hid] = high[part]
            gcat[i * (chunk_rows // BLOCK) + j, :, hid:] = low[part]
        return carry

    lax.fori_loop(0, rows // chunk_rows, project, 0)
    first = node * blocks
    group = 4

    def edges(i, carry):
        hots, messages = [], []
        for k in range(group):
            t = i * group + k
            tile = tiles[t, 0]
            live = tile >= 0
            block = jnp.clip(tile - first, 0, blocks - 1)
            ids = enc_edges[t]
            source = one_hot_rows(ids[0:1])
            target = one_hot_rows(ids[1:2])
            picked = jnp.concatenate([source, target], axis=1)
            table = jnp.concatenate([gcat[block], mcat[...]], axis=0)
            pre = mm(picked, table)
            mh, ml = split(silu(pre[:, :hid] + pre[:, hid:]))
            messages.append(jnp.concatenate([mh, ml], axis=1))
            hots.append(one_hot_cols(jnp.where(live, ids[1:2], -1)))
        acc[...] += mm(jnp.concatenate(hots, axis=1), jnp.concatenate(messages, axis=0))
        return carry

    half_way = slots // group // 2
    lax.fori_loop(0, half_way, edges, 0)
    weight_pass_on(0)
    lax.fori_loop(half_way, slots // group, edges, 0)
    agg_all[me] = acc[:, :hid] + acc[:, hid:]
    for k in range(1, MP):
        y_copy(5, k, agg_all.at[me], agg_all.at[me]).start()
    weight_finish(0)
    weight_pass_on(1)
    for k in range(1, MP):
        y_copy(5, k, agg_all.at[me], agg_all.at[y_from[k]]).wait_recv()
    agg = jnp.concatenate([agg_all[m] for m in range(MP)], axis=1)
    width = mesh_ref.shape[1]
    mesh_one = mesh_ref[...] + product(agg, enc_out_all[...].reshape(width, width))
    normed = norm_rows(mesh_one, gain_one[...])
    own_kv = product(normed, jnp.concatenate([key_w[...], value_w[...]], axis=1))
    here = core * CHIPS + chip
    kv[here] = own_kv

    def link_copy(chunk, pos, slot, step):
        start, size = CHUNKS[chunk]
        piece = kv.at[pos, pl.ds(start, size)]
        return pltpu.make_async_remote_copy(
            src_ref=piece,
            dst_ref=piece,
            send_sem=link_send,
            recv_sem=link_recv.at[chunk, slot],
            device_id={"nodes": chip_node(*step)},
            device_id_type=MESH,
        )

    def core_copy(ref):
        return pltpu.make_async_remote_copy(
            src_ref=ref,
            dst_ref=ref,
            send_sem=core_send,
            recv_sem=core_recv,
            device_id={"nodes": sibling},
            device_id_type=MESH,
        )

    for chunk in range(4):
        for step in onward(chunk, 0, 0):
            link_copy(chunk, here, slot_of(chunk, *step), step).start()
    core_copy(kv.at[here]).start()

    def arrive(event):
        _, _, chunk, dz, dx, slot = event
        pos = core * CHIPS + z_at[-dz] * X + x_at[-dx]
        start, size = CHUNKS[chunk]
        link_copy(chunk, pos, slot, (1, 0)).wait_recv()
        for step in onward(chunk, dz, dx):
            link_copy(
                chunk, pos, slot_of(chunk, dz + step[0], dx + step[1]), step
            ).start()
        core_copy(kv.at[pos, pl.ds(start, size)]).start()

    nh, nl = split(normed)
    uh, ul = split(up_w[...])
    hidden = silu(mm3(nh, nl, uh, ul))
    queue = arrivals()
    near = [e for e in queue if e[0] == 1]
    rest = [e for e in queue if e[0] > 1]
    for event in near:
        arrive(event)
    hh, hl = split(hidden)
    dh, dl = split(down_w[...])
    partial[...] = mm3(hh, hl, dh, dl)
    share = BLOCK // MP

    def share_of(m):
        return pl.ds(pl.multiple_of(m * share, share), share)

    for k in range(1, MP):
        y_copy(6, k, partial.at[share_of(y_at[k])], parts.at[me]).start()
    for item in (2, 3, 4):
        weight_start(item)
    third = len(rest) // 4
    for event in rest[:third]:
        arrive(event)
    weight_finish(1)
    for k in range(1, MP):
        y_copy(6, k, partial.at[share_of(y_at[k])], parts.at[y_from[k]]).wait_recv()
    summed[share_of(me), :] = partial[share_of(me), :] + (
        parts[y_from[1]] + parts[y_from[2]] + parts[y_from[3]]
    )
    for k in range(1, MP):
        y_copy(7, k, summed.at[share_of(me)], summed.at[share_of(me)]).start()
    queries = product(normed, query_w[...]) * (1.0 / math.sqrt(HEAD_DIM))
    for event in rest[third : 2 * third]:
        arrive(event)
    weight_pass_on(2)
    for event in rest[2 * third : 3 * third]:
        arrive(event)
    weight_pass_on(3)
    for event in rest[3 * third :]:
        arrive(event)
    weight_pass_on(4)
    for k in range(1, MP):
        y_copy(7, k, summed.at[share_of(me)], summed.at[share_of(y_from[k])]).wait_recv()
    mesh_mid = mesh_one + summed[...]
    weight_finish(2)
    core_copy(kv.at[pl.ds((1 - core) * CHIPS, CHIPS)]).wait_recv()

    count = lists.shape[1]
    top = jnp.full((BLOCK, 1), -jnp.inf, F32)
    spots = []
    for j in range(count):
        block = lists[node, j]
        spot = jnp.bitwise_and(block, 1) * CHIPS + jnp.right_shift(block, 1)
        spots.append(spot)
        logit = lax.dot_general(
            queries,
            kv[spot][:, :HEAD_DIM],
            (((1,), (1,)), ((), ())),
            precision=FULL,
            preferred_element_type=F32,
        )
        scores[:, j * BLOCK : (j + 1) * BLOCK] = logit
        top = jnp.maximum(top, jnp.max(logit, axis=-1, keepdims=True))
    weight = jnp.exp(scores[...] - top)
    total = jnp.sum(weight, axis=-1, keepdims=True)
    values = jnp.concatenate([kv[spot][:, HEAD_DIM:] for spot in spots], axis=0)
    wh, wl = split(weight)
    vh, vl = split(values)
    att_all[me] = mm3(wh, wl, vh, vl) / total
    for k in range(1, MP):
        y_copy(8, k, att_all.at[me], att_all.at[me]).start()
    weight_finish(3)
    for k in range(1, MP):
        y_copy(8, k, att_all.at[me], att_all.at[y_from[k]]).wait_recv()
    attended = jnp.concatenate([att_all[m] for m in range(MP)], axis=1)
    mesh_two = mesh_mid + product(attended, out_all[...].reshape(width, width))
    normed_two = norm_rows(mesh_two, gain_two[...])
    dec_w = jnp.concatenate([dec_mesh_all[m] for m in range(MP)], axis=1)
    beside[1] = product(normed_two, dec_w)

    def side_copy(way, slot, target):
        return pltpu.make_async_remote_copy(
            src_ref=beside.at[1],
            dst_ref=beside.at[slot],
            send_sem=side_send.at[way],
            recv_sem=side_recv.at[way],
            device_id={"nodes": target},
            device_id_type=MESH,
        )

    side_copy(0, 0, after).start()
    side_copy(1, 2, before).start()
    weight_finish(4)
    core_copy(kv.at[pl.ds(core * CHIPS, CHIPS)]).wait_send()
    link_copy_all = pltpu.make_async_remote_copy(
        src_ref=kv.at[pl.ds(0, CHIPS - 1)],
        dst_ref=kv.at[pl.ds(0, CHIPS - 1)],
        send_sem=link_send,
        recv_sem=link_recv.at[0, 0],
        device_id={"nodes": sibling},
        device_id_type=MESH,
    )
    link_copy_all.wait_send()
    for item, ref in ((5, agg_all.at[me]), (8, att_all.at[me])):
        for k in range(1, MP):
            y_copy(item, k, ref, ref).wait_send()
    for item in (6, 7):
        for k in range(1, MP):
            ref = summed.at[share_of(me)]
            y_copy(item, k, ref, ref).wait_send()
    side_copy(0, 0, after).wait()
    side_copy(1, 2, before).wait()


def mesh_part(tiles, lists, *arrays):
    grid_latent, mesh_latent, enc_grid_w = arrays[:3]
    rows, width = grid_latent.shape
    nodes = mesh_latent.shape[0]
    hid = enc_grid_w.shape[1]
    vmem = pl.BlockSpec(memory_space=pltpu.VMEM)
    smem = pl.BlockSpec(memory_space=pltpu.SMEM)
    dma = pltpu.SemaphoreType.DMA
    listed = lists.shape[1]
    return pl.pallas_call(
        mesh_kernel,
        in_specs=[smem, smem] + [vmem] * len(arrays),
        out_specs=[vmem] * 3,
        out_shape=[
            jax.ShapeDtypeStruct((3, nodes, width), F32),
            jax.ShapeDtypeStruct((MP, width, hid), F32),
            jax.ShapeDtypeStruct((MP, hid, width), F32),
        ],
        scratch_shapes=[
            pltpu.VMEM((width, 2 * hid), BF16),
            pltpu.VMEM((rows // BLOCK, BLOCK, 2 * hid), BF16),
            pltpu.VMEM((nodes, 2 * hid), BF16),
            pltpu.VMEM((nodes, 2 * hid), F32),
            pltpu.VMEM((MP, nodes, hid), F32),
            pltpu.VMEM((MP, hid, width), F32),
            pltpu.VMEM((MP, hid, width), F32),
            pltpu.VMEM((MP, width, hid), F32),
            pltpu.VMEM((2 * CHIPS, nodes, 2 * HEAD_DIM), F32),
            pltpu.VMEM((nodes, width), F32),
            pltpu.VMEM((MP, nodes // MP, width), F32),
            pltpu.VMEM((nodes, width), F32),
            pltpu.VMEM((MP, nodes, HEAD_DIM), F32),
            pltpu.VMEM((nodes, listed * BLOCK), F32),
            dma((9, MP - 1)),
            dma((9, MP - 1)),
            dma((5, MP - 1)),
            dma((5, MP - 1)),
            dma(()),
            dma((4, CHIPS)),
            dma(()),
            dma(()),
            dma((2,)),
            dma((2,)),
        ],
        compiler_params=pltpu.CompilerParams(
            collective_id=0, has_side_effects=True, vmem_limit_bytes=52 << 20
        ),
        name="mesh_part",
    )(tiles, lists, *arrays)


def exchange_kernel(rows_ref, out_ref, send, recv, local):
    me = lax.axis_index("mp")
    share = rows_ref.shape[1]
    y_at = [lax.rem(me + k, MP) for k in range(MP)]
    y_from = [lax.rem(me + MP - k, MP) for k in range(MP)]
    barrier = pltpu.get_barrier_semaphore()
    for k in range(1, MP):
        pl.semaphore_signal(barrier, inc=1, device_id={"mp": y_at[k]}, device_id_type=MESH)
    pl.semaphore_wait(barrier, MP - 1)

    def place(m):
        return pl.ds(pl.multiple_of(m * share, share), share)

    def copy(k, at):
        return pltpu.make_async_remote_copy(
            src_ref=rows_ref.at[y_at[k]],
            dst_ref=out_ref.at[place(at)],
            send_sem=send.at[k - 1],
            recv_sem=recv.at[k - 1],
            device_id={"mp": y_at[k]},
            device_id_type=MESH,
        )

    for k in (2, 1, 3):
        copy(k, me).start()
    own = pltpu.make_async_copy(rows_ref.at[me], out_ref.at[place(me)], local)
    own.start()
    own.wait()
    for k in range(1, MP):
        copy(k, y_from[k]).wait_recv()
        copy(k, me).wait_send()


def exchange(rows):
    dma = pltpu.SemaphoreType.DMA
    anywhere = pl.BlockSpec(memory_space=pl.ANY)
    return pl.pallas_call(
        exchange_kernel,
        in_specs=[anywhere],
        out_specs=anywhere,
        out_shape=jax.ShapeDtypeStruct((MP * rows.shape[1], rows.shape[2]), F32),
        scratch_shapes=[dma((MP - 1,)), dma((MP - 1,)), dma(())],
        compiler_params=pltpu.CompilerParams(collective_id=1, has_side_effects=True),
        name="exchange",
    )(rows)


def decoder_kernel(
    tiles, grid_ref, wg_ref, mesh_ref, wo_ref, edges_ref, out_ref, gcat, mcat, wcat, agg
):
    rows, width = grid_ref.shape
    hid = width
    blocks = rows // BLOCK
    mp = lax.axis_size("mp")
    node = lax.axis_index("nodes")
    nodes = lax.axis_size("nodes")
    first = (node * mp + lax.axis_index("mp")) * blocks

    wh, wl = split(jnp.concatenate([wg_ref[m] for m in range(MP)], axis=1))
    wcat[:, :hid] = wh
    wcat[:, hid:] = wl
    for b in range(blocks):
        here = slice(b * BLOCK, (b + 1) * BLOCK)
        xh, xl = split(grid_ref[here, :])
        high, low = split(mm(xh, wcat[:, :hid]) + mm(xh, wcat[:, hid:]) + mm(xl, wcat[:, :hid]))
        gcat[here, :hid] = high
        gcat[here, hid:] = low
    high, low = split(mesh_ref[...].reshape(-1, width))
    mcat[:, :hid] = high
    mcat[:, hid:] = low
    agg[...] = jnp.zeros_like(agg)

    def body(t, carry):
        block = tiles[t, 1] - first

        @pl.when(jnp.logical_and(block >= 0, block < blocks))
        def _():
            beside = lax.rem(tiles[t, 0] - (node - 1) + nodes, nodes)
            ids = edges_ref[t]
            source = one_hot_rows(ids[0:1])
            target = one_hot_rows(ids[1:2])
            picked = jnp.concatenate([source, target], axis=1)
            here = pl.ds(pl.multiple_of(block * BLOCK, BLOCK), BLOCK)
            there = pl.ds(pl.multiple_of(beside * BLOCK, BLOCK), BLOCK)
            table = jnp.concatenate([mcat[there, :], gcat[here, :]], axis=0)
            pre = mm(picked, table)
            mh, ml = split(silu(pre[:, :hid] + pre[:, hid:]))
            hot = one_hot_cols(ids[1:2])
            agg[here, :] += mm(hot, mh) + mm(hot, ml)

        return carry

    lax.fori_loop(0, edges_ref.shape[0], body, 0)
    wh, wl = split(wo_ref[...].reshape(hid, width))
    for b in range(blocks):
        here = slice(b * BLOCK, (b + 1) * BLOCK)
        ah, al = split(agg[here, :])
        done = grid_ref[here, :] + mm3(ah, al, wh, wl)
        for m in range(MP):
            out_ref[m, here, :] = done[:, m * (width // MP) : (m + 1) * (width // MP)]


def decoder(grid_latent, dec_grid_w, mesh_beside, dec_out_w, dec_tiles, dec_edges):
    rows, width = grid_latent.shape
    hid = width
    vmem = pl.BlockSpec(memory_space=pltpu.VMEM)
    share = rows // lax.axis_size("mp")
    me = lax.axis_index("mp")
    mine = lax.dynamic_slice_in_dim(grid_latent, me * share, share, 0)
    return pl.pallas_call(
        decoder_kernel,
        in_specs=[pl.BlockSpec(memory_space=pltpu.SMEM)] + [vmem] * 5,
        out_specs=vmem,
        out_shape=jax.ShapeDtypeStruct((MP, share, width // MP), F32),
        scratch_shapes=[
            pltpu.VMEM((share, 2 * hid), BF16),
            pltpu.VMEM((3 * BLOCK, 2 * hid), BF16),
            pltpu.VMEM((width, 2 * hid), BF16),
            pltpu.VMEM((share, hid), F32),
        ],
        compiler_params=pltpu.CompilerParams(vmem_limit_bytes=40 << 20),
        cost_estimate=pl.CostEstimate(
            flops=2 * 6 * share * width * hid, bytes_accessed=6 << 20, transcendentals=1 << 20
        ),
        name="decoder",
    )(dec_tiles, mine, dec_grid_w, mesh_beside, dec_out_w, dec_edges)


def per_device(
    grid_latent,
    mesh_latent,
    enc_grid_w,
    enc_mesh_w,
    enc_out_w,
    block_gain,
    query_w,
    key_w,
    value_w,
    out_w,
    up_w,
    down_w,
    dec_gain,
    dec_grid_w,
    dec_mesh_w,
    dec_out_w,
    neighbor_blocks,
    enc_tiles,
    enc_edges,
    dec_tiles,
    dec_edges,
):
    beside, dec_grid_all, dec_out_all = mesh_part(
        enc_tiles,
        neighbor_blocks,
        grid_latent,
        mesh_latent,
        enc_grid_w,
        enc_mesh_w,
        enc_edges,
        enc_out_w,
        block_gain[None],
        query_w,
        key_w,
        value_w,
        out_w,
        up_w,
        down_w,
        dec_gain[None],
        dec_grid_w,
        dec_mesh_w,
        dec_out_w,
    )
    rows = decoder(grid_latent, dec_grid_all, beside, dec_out_all, dec_tiles, dec_edges)
    return exchange(rows)


def solution(mesh):
    in_specs = (
        P("nodes", None),
        P("nodes", None),
        P(None, "mp"),
        P(None, "mp"),
        P("mp", None),
        P(),
        P(None, "mp"),
        P(None, "mp"),
        P(None, "mp"),
        P("mp", None),
        P(None, "mp"),
        P("mp", None),
        P(),
        P(None, "mp"),
        P(None, "mp"),
        P("mp", None),
        P(),
        P("nodes", None),
        P("nodes", None, None),
        P("nodes", None),
        P("nodes", None, None),
    )
    out_specs = P("nodes", "mp")
    return jax.shard_map(
        per_device, mesh=mesh, in_specs=in_specs, out_specs=out_specs, check_vma=False
    )
```

time: 303 us -> 129 us (0.43)
  waiting for transfers between devices: 172 us -> 0 us
  Pallas kernels: 29.2 us -> 109 us
  blocking collectives: 42.2 us -> 0 us
  between operations: 13.4 us -> 0.07 us
  matrix products: 9.96 us -> 0 us
  local copies, waits for them, and re-layouts: 25.1 us -> 19.2 us
  other arithmetic: 5.12 us -> 0 us
    all_gather x4 -> x0, waiting for transfers between devices: 151 us -> none  [the longest x1 82.7 us: per_device(): everything = lax.all_gather(key_values, 'nodes', axis=0, tiled=False)]
    pallas_call x2, Pallas kernels: 15.8 us -> 96.8 us  [the longest x1 81 us: mesh_part(): pl.pallas_call(mesh_kernel, in_specs=[smem, smem] + [vmem] * len(arrays),...]
    all_gather x2 -> x0, blocking collectives: 22.7 us -> none  [the longest x1 12.3 us: per_device(): enc_agg = lax.all_gather(enc_agg, 'mp', axis=1, tiled=True)]
    all_to_all x1 -> x0, blocking collectives: 19.5 us -> none  [per_device(): lax.all_to_all(rows_out, 'mp', split_axis=1, concat_axis=0, tiled=True)]
    psum x1 -> x0, waiting for transfers between devices: 16.8 us -> none  [per_device(): mlp = lax.psum(product(hidden, down_w), 'mp')]
    dot_general x8 -> x0, matrix products: 9.96 us -> none  [product(): return jnp.dot(matrix, weight, precision=FULL, preferred_element_type=F32)]
    all_gather x1 -> x0, local copies, waits for them, and re-layouts: 8.98 us -> none  [per_device(): everything = lax.all_gather(key_values, 'nodes', axis=0, tiled=False)]
    concatenate x3 -> x0, other arithmetic: 4.74 us -> none  [the longest x1 2.14 us: per_device(): outs = jnp.concatenate([enc_out_w, out_w, dec_out_w], axis=1)]
  transfers between devices with their start and end apart: 7 -> 0, of which waited for: 7 -> 0; matrix products, arithmetic and copies ran while one was open for 7% -> 0% of each run, Pallas kernels for 5% -> 0%
where the time goes in v2:
time: 129 us; the launch traced here: 128 us
  Pallas kernels  109 us (84%)
  local copies, waits for them, and re-layouts  19.2 us (15%)
    pallas_call x1, Pallas kernels, mesh_part(): pl.pallas_call(mesh_kernel, in_specs=[smem, smem] + [vmem] * len(arrays),...  81 us
    unnamed x34, local copies, waits for them, and re-layouts  17.9 us
    pallas_call x1, Pallas kernels, exchange(): pl.pallas_call(exchange_kernel, in_specs=[anywhere], out_specs=anywhere,...  15.8 us
    pallas_call x1, Pallas kernels, decoder(): pl.pallas_call(decoder_kernel, in_specs=[pl.BlockSpec(memory_space=pltpu....  12 us

profile of v2, /device:TPU:3, one launch (start us, length us, event | category | flops | bytes accessed | tf_op | source)
XLA Modules:
  0.0 128.0 jit_solution(6189515966511054128)
XLA Ops:
  0.0 0.8 copy.22.tiles
  0.8 0.8 copy.24.tiles
  1.5 0.8 copy.23.lists
  2.3 1.3 %constant_dynamic-slice_fusion.grid_ref = f32[512,512]{1,0:T(8,128)S(1)} fusion(f32[2048,512]{1,0:T(8,128)} %grid_ref.1, s32[]{:T(128)S(6)} %select_n.3), kind=kLoop, calls=%fused_computation | loop fusion | bytes 2097156 | tf_op jit(solution)/shard_map/dynamic_slice | solution.py:633
  3.6 0.0 copy-start.1
  3.6 0.9 copy-done.1
  4.6 0.9 copy-done.2
  5.5 0.9 copy-done.3
  6.5 0.9 copy-done.4
  7.4 0.9 copy-done.5
  8.4 0.9 copy-done.6
  9.3 0.9 copy-done.7
  10.3 0.8 copy-done.8
  11.0 0.7 copy-done.9
  11.7 0.7 copy-done.10
  12.4 81.0 %mesh_part.1 = (f32[3,128,512]{2,1,0:T(8,128)}, f32[4,512,128]{2,1,0:T(8,128)}, f32[4,128,512]{2,1,0:T(8,128)}) custom-call(s32[32,2]{1,0:T(8,128)S(1)} %copy.22.tiles, s32[64,16]{1,0:T(8,128)S(1)} %copy.23.lists, f32[2048,512]{1,0:T(8,128)} %grid_ref.1, f32[128,512]{1,0:T(8,128)S(1)} %copy-done.1, f32[512,128]{1,0:T(8,128)S(1)} %copy-done.2, ...), custom_call_target="tpu_custom_call" | custom-call | tf_op jit(solution)/shard_map/mesh_part/pallas_call | solution.py:483
  93.4 1.2 copy-done.11
  94.6 1.2 copy-done.12
  95.9 1.1 copy-done.13
  97.0 12.0 %decoder.1.rows_ref = f32[4,512,128]{2,1,0:T(8,128)S(1)} custom-call(s32[48,2]{1,0:T(8,128)S(1)} %copy.24.tiles, f32[512,512]{1,0:T(8,128)S(1)} %constant_dynamic-slice_fusion.grid_ref, f32[4,512,128]{2,1,0:T(8,128)S(1)} %copy-done.11, f32[3,128,512]{2,1,0:T(8,128)S(1)} %copy-done.13, f32[4,128,512]{2,1,0:T(8,128)S(1)} %copy-done.12, ...), custom_call_target="tpu_custom_call" | custom-call | flops 1610612736 | bytes 6291456 | tf_op jit(solution)/shard_map/decoder/pallas_call | solution.py:634
  109.0 0.0 copy-start
  109.0 1.0 copy-done
  110.0 15.8 %exchange.1 = f32[2048,128]{1,0:T(8,128)} custom-call(f32[4,512,128]{2,1,0:T(8,128)} %copy-done), custom_call_target="tpu_custom_call" | custom-call | tf_op jit(solution)/shard_map/exchange/pallas_call | solution.py:561
  125.8 2.3 %copy.26 = f32[2048,128]{1,0:T(8,128)} copy(f32[2048,128]{1,0:T(8,128)} %exchange.1) | data formatting | bytes 2097152
  (14 shorter events, 0.0 us)
Async XLA Ops:
  3.6 1.0 copy-start.1
  4.6 0.9 copy-start.2
  5.5 0.9 copy-start.3
  6.5 0.9 copy-start.4
  7.4 0.9 copy-start.5
  8.4 0.9 copy-start.6
  9.3 0.9 copy-start.7
  10.3 0.8 copy-start.8
  11.0 0.7 copy-start.9
  11.7 0.7 copy-start.10
  12.4 81.0 %copy-start.14 = (s32[48,2,128]{2,1,0:T(2,128)S(1)}, s32[48,2,128]{2,1,0:T(2,128)}, u32[]{:S(2)}) copy-start(s32[48,2,128]{2,1,0:T(2,128)} %edges_ref.1) | copy-start | bytes 147460
  93.4 1.2 copy-start.11
  94.6 1.2 copy-start.12
  95.9 1.1 copy-start.13
  109.0 1.0 copy-start

commit v3 on v2

v3 whole, which is shorter than its diff:
```python
import math

import jax
import jax.numpy as jnp
from jax import lax
from jax.experimental import pallas as pl
from jax.experimental.pallas import tpu as pltpu
from jax.sharding import PartitionSpec as P

HEAD_DIM = 128
BLOCK = 128
FULL = lax.Precision.HIGHEST
F32 = jnp.float32
BF16 = jnp.bfloat16


def product(matrix, weight):
    return jnp.dot(matrix, weight, precision=FULL, preferred_element_type=F32)


def split(x):
    high = x.astype(BF16)
    low = (x - high.astype(F32)).astype(BF16)
    return high, low


def mm(a, b):
    return jnp.dot(a, b, preferred_element_type=F32)


def mm_first(a, b):
    return lax.dot_general(a, b, (((0,), (0,)), ((), ())), preferred_element_type=F32)


def silu(v):
    half = 0.5 * v
    return half + half * jnp.tanh(half)


def one_hot_cols(row):
    sub = lax.broadcasted_iota(jnp.int32, (BLOCK, BLOCK), 0)
    return jnp.where(row == sub, 1.0, 0.0).astype(BF16)


MESH = pl.DeviceIdType.MESH
Z, X, MP = 8, 4, 4
CHIPS = Z * X
CHUNKS = ((0, 72), (72, 56))


def spans(chunk):
    return (1 - Z // 2, Z // 2), (1 - X // 2, X // 2)


def onward(chunk, dz, dx):
    zs, xs = spans(chunk)
    steps = []

    def along_z(start):
        if dz >= 0 and dz + 1 <= zs[1] and (start or dz > 0):
            steps.append((1, 0))
        if dz <= 0 and dz - 1 >= zs[0] and (start or dz < 0):
            steps.append((-1, 0))

    def along_x(start):
        if dx >= 0 and dx + 1 <= xs[1] and (start or dx > 0):
            steps.append((0, 1))
        if dx <= 0 and dx - 1 >= xs[0] and (start or dx < 0):
            steps.append((0, -1))

    if chunk == 0:
        if dx == 0:
            along_z(dz == 0)
            along_x(True)
        else:
            along_x(False)
    else:
        if dz == 0:
            along_x(dx == 0)
            along_z(True)
        else:
            along_z(False)
    return sorted(steps, key=lambda step: not branching(chunk, step))


def arrivals():
    events = []
    for chunk in range(len(CHUNKS)):
        zs, xs = spans(chunk)
        for dz in range(zs[0], zs[1] + 1):
            for dx in range(xs[0], xs[1] + 1):
                if (dz, dx) != (0, 0):
                    first, second = (dz, dx) if chunk == 0 else (dx, dz)
                    order = (abs(dz) + abs(dx), second != 0, abs(second))
                    events.append((order, chunk, dz, dx, slot_of(chunk, dz, dx)))
    return sorted(events)


def branching(chunk, step):
    return (step[0] != 0) == (chunk == 0)


def slot_of(chunk, dz, dx):
    zs, xs = spans(chunk)
    return (dz - zs[0]) * X + dx - xs[0]


def norm_rows(x, gain):
    centre = jnp.mean(x, axis=-1, keepdims=True)
    shifted = x - centre
    spread = jnp.mean(shifted * shifted, axis=-1, keepdims=True)
    return shifted * lax.rsqrt(spread + 1e-05) * gain


def mm3(ah, al, bh, bl):
    return mm(ah, bh) + mm(ah, bl) + mm(al, bh)


FETCHED = (
    "enc_grid_w",
    "mesh_latent",
    "enc_mesh_w",
    "enc_edges",
    "enc_out_w",
    "dec_grid_w",
    "block_gain",
    "key_w",
    "value_w",
    "up_w",
    "down_w",
    "query_w",
    "out_w",
    "dec_mesh_w",
    "dec_out_w",
    "dec_gain",
)


def mesh_kernel(tiles, lists, order, grid_hbm, *refs):
    count = len(FETCHED)
    given = dict(zip(FETCHED, refs[:count]))
    beside, gdec, dec_out_all = refs[count : count + 3]
    rest = refs[count + 3 :]
    held = dict(zip(FETCHED, rest[:count]))
    (
        grid_ref,
        wcat,
        gcat,
        mcat,
        acc,
        agg_all,
        enc_out_all,
        out_all,
        dec_mesh_all,
        dec_grid_all,
        kv,
        partial,
        parts,
        summed,
        att_all,
        scores,
        fetch_sem,
        grid_sem,
        y_send,
        y_recv,
        c_send,
        c_recv,
        link_send,
        link_recv,
        core_send,
        core_recv,
        side_send,
        side_recv,
    ) = rest[count:]
    chunk_rows = 256

    def fetch(name):
        return pltpu.make_async_copy(
            given[name], held[name], fetch_sem.at[FETCHED.index(name)]
        )

    def fetch_rows(i):
        here = pl.ds(pl.multiple_of(i * chunk_rows, chunk_rows), chunk_rows)
        there = pl.ds(i * (chunk_rows // BLOCK), chunk_rows // BLOCK)
        return pltpu.make_async_copy(
            grid_hbm.at[here].reshape(chunk_rows // BLOCK, BLOCK, grid_hbm.shape[1]),
            grid_ref.at[there],
            grid_sem.at[i],
        )

    for name in FETCHED[:3]:
        fetch(name).start()
    for i in range(grid_hbm.shape[0] // chunk_rows):
        fetch_rows(i).start()
    for name in FETCHED[3:]:
        fetch(name).start()

    def got(name):
        fetch(name).wait()
        return held[name][...]

    me = lax.axis_index("mp")
    node = lax.axis_index("nodes")
    nodes = Z * X * 2
    core = lax.rem(node, 2)
    chip = node // 2
    z, x = chip // X, lax.rem(chip, X)
    way = 1 - 2 * core
    z_at = {d: lax.rem(z + way * d + Z, Z) for d in range(-4, 5)}
    x_at = {d: lax.rem(x + way * d + X, X) for d in range(-2, 3)}
    sibling = node + way
    y_at = [lax.rem(me + k, MP) for k in range(MP)]
    y_from = [lax.rem(me + MP - k, MP) for k in range(MP)]
    after, before = lax.rem(node + 1, nodes), lax.rem(node + nodes - 1, nodes)
    beyond = jnp.where(core == 0, before, after)

    def chip_node(dz, dx):
        return (z_at[dz] * X + x_at[dx]) * 2 + core

    barrier = pltpu.get_barrier_semaphore()
    for dz, dx in ((1, 0), (-1, 0), (0, 1), (0, -1)):
        pl.semaphore_signal(
            barrier, inc=1, device_id={"nodes": chip_node(dz, dx)}, device_id_type=MESH
        )
    pl.semaphore_signal(barrier, inc=1, device_id={"nodes": sibling}, device_id_type=MESH)
    pl.semaphore_signal(barrier, inc=1, device_id={"nodes": beyond}, device_id_type=MESH)
    for k in range(1, MP):
        pl.semaphore_signal(barrier, inc=1, device_id={"mp": y_at[k]}, device_id_type=MESH)
    pl.semaphore_wait(barrier, 9)

    def y_copy(item, k, src, dst):
        return pltpu.make_async_remote_copy(
            src_ref=src,
            dst_ref=dst,
            send_sem=y_send.at[item, k - 1],
            recv_sem=y_recv.at[item, k - 1],
            device_id={"mp": y_at[k]},
            device_id_type=MESH,
        )

    def c_copy(item, k, ref):
        return pltpu.make_async_remote_copy(
            src_ref=ref,
            dst_ref=ref,
            send_sem=c_send.at[item, k - 1],
            recv_sem=c_recv.at[item, k - 1],
            device_id={"nodes": sibling},
            device_id_type=MESH,
        )

    weights = {
        0: ("enc_out_w", enc_out_all),
        1: ("dec_grid_w", dec_grid_all),
        2: ("out_w", out_all),
        3: ("dec_mesh_w", dec_mesh_all),
        4: ("dec_out_w", dec_out_all),
    }

    def halves(item):
        half = given[weights[item][0]].shape[0] // 2
        return pl.ds(pl.multiple_of(core * half, half), half), pl.ds(
            pl.multiple_of((1 - core) * half, half), half
        )

    def weight_start(item):
        name, whole = weights[item]
        own = given[name]
        mine, _ = halves(item)
        for k in range(1, MP):
            y_copy(item, k, own.at[mine], whole.at[me, mine]).start()

    def weight_pass_on(item):
        name, whole = weights[item]
        own = given[name]
        mine, _ = halves(item)
        for k in range(1, MP):
            y_copy(item, k, own.at[mine], whole.at[y_from[k], mine]).wait_recv()
            c_copy(item, k, whole.at[y_from[k], mine]).start()

    def weight_finish(item):
        name, whole = weights[item]
        own = given[name]
        mine, other = halves(item)
        whole[me] = got(name)
        for k in range(1, MP):
            c_copy(item, k, whole.at[y_from[k], other]).wait_recv()
        for k in range(1, MP):
            y_copy(item, k, own.at[mine], whole.at[me, mine]).wait_send()
            c_copy(item, k, whole.at[y_from[k], mine]).wait_send()

    weight_start(0)

    rows, hid = grid_hbm.shape[0], given["enc_grid_w"].shape[1]
    blocks = rows // BLOCK
    enc_edges = held["enc_edges"]
    slots = enc_edges.shape[0]
    high, low = split(got("enc_grid_w"))
    wcat[:, :hid] = high
    wcat[:, hid:] = low
    high, low = split(product(got("mesh_latent"), got("enc_mesh_w")))
    mcat[:, :hid] = high
    mcat[:, hid:] = low
    acc[...] = jnp.zeros_like(acc)

    def project(i, carry):
        fetch_rows(i).wait()
        there = pl.ds(i * (chunk_rows // BLOCK), chunk_rows // BLOCK)
        xh, xl = split(grid_ref[there].reshape(chunk_rows, -1))
        both = mm(xh, wcat[...]) + mm(xl, wcat[...])
        high, low = split(both[:, :hid] + both[:, hid:])
        for j in range(chunk_rows // BLOCK):
            part = slice(j * BLOCK, (j + 1) * BLOCK)
            gcat[i * (chunk_rows // BLOCK) + j, :, :hid] = high[part]
            gcat[i * (chunk_rows // BLOCK) + j, :, hid:] = low[part]
        return carry

    lax.fori_loop(0, rows // chunk_rows, project, 0)
    first = node * blocks
    group = 8

    def edges(i, carry):
        hots, messages = [], []
        for k in range(group):
            t = i * group + k
            tile = tiles[0, t]
            live = tile >= 0
            block = jnp.clip(tile - first, 0, blocks - 1)
            ids = enc_edges[t]
            target = one_hot_cols(ids[1:2])
            picked = jnp.concatenate([one_hot_cols(ids[0:1]), target], axis=0)
            table = jnp.concatenate([gcat[block], mcat[...]], axis=0)
            pre = mm_first(picked, table)
            mh, ml = split(silu(pre[:, :hid] + pre[:, hid:]))
            messages.append(jnp.concatenate([mh, ml], axis=1))
            hots.append(one_hot_cols(jnp.where(live, ids[1:2], -1)))
        acc[...] += mm(jnp.concatenate(hots, axis=1), jnp.concatenate(messages, axis=0))
        return carry

    half_way = slots // group // 2
    fetch("enc_edges").wait()
    lax.fori_loop(0, half_way, edges, 0)
    weight_pass_on(0)
    lax.fori_loop(half_way, slots // group, edges, 0)
    agg_all[me] = acc[:, :hid] + acc[:, hid:]
    for k in range(1, MP):
        y_copy(5, k, agg_all.at[me], agg_all.at[me]).start()
    weight_finish(0)
    for k in range(1, MP):
        y_copy(5, k, agg_all.at[me], agg_all.at[y_from[k]]).wait_recv()
    agg = jnp.concatenate([agg_all[m] for m in range(MP)], axis=1)
    width = grid_hbm.shape[1]
    mesh_one = held["mesh_latent"][...] + product(agg, enc_out_all[...].reshape(width, width))
    normed = norm_rows(mesh_one, got("block_gain"))
    own_kv = product(normed, jnp.concatenate([got("key_w"), got("value_w")], axis=1))
    here = core * CHIPS + chip
    kv[here] = own_kv

    def link_copy(chunk, pos, slot, step):
        start, size = CHUNKS[chunk]
        piece = kv.at[pos, pl.ds(start, size)]
        return pltpu.make_async_remote_copy(
            src_ref=piece,
            dst_ref=piece,
            send_sem=link_send,
            recv_sem=link_recv.at[chunk, slot],
            device_id={"nodes": chip_node(*step)},
            device_id_type=MESH,
        )

    def core_copy(ref):
        return pltpu.make_async_remote_copy(
            src_ref=ref,
            dst_ref=ref,
            send_sem=core_send,
            recv_sem=core_recv,
            device_id={"nodes": sibling},
            device_id_type=MESH,
        )

    starts = [(chunk, step) for chunk in range(len(CHUNKS)) for step in onward(chunk, 0, 0)]
    for chunk, step in sorted(starts, key=lambda s: not branching(*s)):
        link_copy(chunk, here, slot_of(chunk, *step), step).start()
    core_copy(kv.at[here]).start()
    weight_start(1)

    def arrive(event):
        _, chunk, dz, dx, slot = event
        pos = core * CHIPS + z_at[-dz] * X + x_at[-dx]
        start, size = CHUNKS[chunk]
        link_copy(chunk, pos, slot, (1, 0)).wait_recv()
        for step in onward(chunk, dz, dx):
            link_copy(
                chunk, pos, slot_of(chunk, dz + step[0], dx + step[1]), step
            ).start()
        core_copy(kv.at[pos, pl.ds(start, size)]).start()

    nh, nl = split(normed)
    uh, ul = split(got("up_w"))
    hidden = silu(mm3(nh, nl, uh, ul))
    queue = arrivals()
    near = [e for e in queue if e[0][0] == 1]
    rest = [e for e in queue if e[0][0] > 1]
    assert gdec.shape[0] == 4 * BLOCK
    for event in near:
        arrive(event)
    hh, hl = split(hidden)
    dh, dl = split(got("down_w"))
    partial[...] = mm3(hh, hl, dh, dl)
    share = BLOCK // MP

    def share_of(m):
        return pl.ds(pl.multiple_of(m * share, share), share)

    for k in range(1, MP):
        y_copy(6, k, partial.at[share_of(y_at[k])], parts.at[me]).start()
    for item in (2, 3, 4):
        weight_start(item)
    weight_pass_on(1)
    rest_count = len(rest)
    third = rest_count // 4
    for event in rest[:third]:
        arrive(event)
    weight_finish(1)
    gh, gl = split(jnp.concatenate([dec_grid_all[m] for m in range(MP)], axis=1))

    def grid_decode(b):
        block = jnp.clip(order[0, me * MP + b], 0, blocks - 1)
        xh, xl = split(grid_ref[block])
        high, low = split(mm3(xh, xl, gh, gl))
        gdec[b * BLOCK : (b + 1) * BLOCK, :width] = high
        gdec[b * BLOCK : (b + 1) * BLOCK, width:] = low

    grid_decode(0)
    for k in range(1, MP):
        y_copy(6, k, partial.at[share_of(y_at[k])], parts.at[y_from[k]]).wait_recv()
    summed[share_of(me), :] = partial[share_of(me), :] + (
        parts[y_from[1]] + parts[y_from[2]] + parts[y_from[3]]
    )
    for k in range(1, MP):
        y_copy(7, k, summed.at[share_of(me)], summed.at[share_of(me)]).start()
    queries = product(normed, got("query_w")) * (1.0 / math.sqrt(HEAD_DIM))
    for event in rest[third : 2 * third]:
        arrive(event)
    grid_decode(1)
    weight_pass_on(2)
    for event in rest[2 * third : 3 * third]:
        arrive(event)
    grid_decode(2)
    weight_pass_on(3)
    for event in rest[3 * third :]:
        arrive(event)
    weight_pass_on(4)
    grid_decode(3)
    for k in range(1, MP):
        y_copy(7, k, summed.at[share_of(me)], summed.at[share_of(y_from[k])]).wait_recv()
    mesh_mid = mesh_one + summed[...]
    weight_finish(2)
    core_copy(kv.at[pl.ds((1 - core) * CHIPS, CHIPS)]).wait_recv()

    count = lists.shape[0]
    top = jnp.full((BLOCK, 1), -jnp.inf, F32)
    spots = []
    for j in range(count):
        block = lists[j, node]
        spot = jnp.bitwise_and(block, 1) * CHIPS + jnp.right_shift(block, 1)
        spots.append(spot)
        logit = lax.dot_general(
            queries,
            kv[spot][:, :HEAD_DIM],
            (((1,), (1,)), ((), ())),
            precision=FULL,
            preferred_element_type=F32,
        )
        scores[:, j * BLOCK : (j + 1) * BLOCK] = logit
        top = jnp.maximum(top, jnp.max(logit, axis=-1, keepdims=True))
    weight = jnp.exp(scores[...] - top)
    total = jnp.sum(weight, axis=-1, keepdims=True)
    values = jnp.concatenate([kv[spot][:, HEAD_DIM:] for spot in spots], axis=0)
    wh, wl = split(weight)
    vh, vl = split(values)
    att_all[me] = mm3(wh, wl, vh, vl) / total
    for k in range(1, MP):
        y_copy(8, k, att_all.at[me], att_all.at[me]).start()
    weight_finish(3)
    for k in range(1, MP):
        y_copy(8, k, att_all.at[me], att_all.at[y_from[k]]).wait_recv()
    attended = jnp.concatenate([att_all[m] for m in range(MP)], axis=1)
    mesh_two = mesh_mid + mm3(*split(attended), *split(out_all[...].reshape(width, width)))
    normed_two = norm_rows(mesh_two, got("dec_gain"))
    dec_w = jnp.concatenate([dec_mesh_all[m] for m in range(MP)], axis=1)
    beside[1] = mm3(*split(normed_two), *split(dec_w))

    def side_copy(way, slot, target):
        return pltpu.make_async_remote_copy(
            src_ref=beside.at[1],
            dst_ref=beside.at[slot],
            send_sem=side_send.at[way],
            recv_sem=side_recv.at[way],
            device_id={"nodes": target},
            device_id_type=MESH,
        )

    side_copy(0, 0, after).start()
    side_copy(1, 2, before).start()
    weight_finish(4)
    core_copy(kv.at[pl.ds(core * CHIPS, CHIPS)]).wait_send()
    link_copy_all = pltpu.make_async_remote_copy(
        src_ref=kv.at[pl.ds(0, CHIPS - 1)],
        dst_ref=kv.at[pl.ds(0, CHIPS - 1)],
        send_sem=link_send,
        recv_sem=link_recv.at[0, 0],
        device_id={"nodes": sibling},
        device_id_type=MESH,
    )
    link_copy_all.wait_send()
    for item, ref in ((5, agg_all.at[me]), (8, att_all.at[me])):
        for k in range(1, MP):
            y_copy(item, k, ref, ref).wait_send()
    for item in (6, 7):
        for k in range(1, MP):
            ref = summed.at[share_of(me)]
            y_copy(item, k, ref, ref).wait_send()
    side_copy(0, 0, after).wait()
    side_copy(1, 2, before).wait()


def mesh_part(tiles, lists, order, grid_latent, arrays):
    rows, width = grid_latent.shape
    nodes = arrays["mesh_latent"].shape[0]
    hid = arrays["enc_grid_w"].shape[1]
    vmem = pl.BlockSpec(memory_space=pltpu.VMEM)
    smem = pl.BlockSpec(memory_space=pltpu.SMEM)
    hbm = pl.BlockSpec(memory_space=pltpu.HBM)
    dma = pltpu.SemaphoreType.DMA
    listed = lists.shape[0]
    operands = [arrays[name] for name in FETCHED]
    return pl.pallas_call(
        mesh_kernel,
        in_specs=[smem, smem, smem, hbm] + [hbm] * len(operands),
        out_specs=[vmem] * 3,
        out_shape=[
            jax.ShapeDtypeStruct((3, nodes, width), F32),
            jax.ShapeDtypeStruct((rows // MP, 2 * width), BF16),
            jax.ShapeDtypeStruct((MP, hid, width), F32),
        ],
        scratch_shapes=[pltpu.VMEM(array.shape, array.dtype) for array in operands]
        + [
            pltpu.VMEM((rows // BLOCK, BLOCK, width), F32),
            pltpu.VMEM((width, 2 * hid), BF16),
            pltpu.VMEM((rows // BLOCK, BLOCK, 2 * hid), BF16),
            pltpu.VMEM((nodes, 2 * hid), BF16),
            pltpu.VMEM((nodes, 2 * hid), F32),
            pltpu.VMEM((MP, nodes, hid), F32),
            pltpu.VMEM((MP, hid, width), F32),
            pltpu.VMEM((MP, hid, width), F32),
            pltpu.VMEM((MP, width, hid), F32),
            pltpu.VMEM((MP, width, hid), F32),
            pltpu.VMEM((2 * CHIPS, nodes, 2 * HEAD_DIM), F32),
            pltpu.VMEM((nodes, width), F32),
            pltpu.VMEM((MP, nodes // MP, width), F32),
            pltpu.VMEM((nodes, width), F32),
            pltpu.VMEM((MP, nodes, HEAD_DIM), F32),
            pltpu.VMEM((nodes, listed * BLOCK), F32),
            dma((len(operands),)),
            dma((rows // 256,)),
            dma((9, MP - 1)),
            dma((9, MP - 1)),
            dma((5, MP - 1)),
            dma((5, MP - 1)),
            dma(()),
            dma((len(CHUNKS), CHIPS)),
            dma(()),
            dma(()),
            dma((2,)),
            dma((2,)),
        ],
        compiler_params=pltpu.CompilerParams(
            collective_id=0, has_side_effects=True, vmem_limit_bytes=62 << 20
        ),
        name="mesh_part",
    )(tiles, lists, order, grid_latent, *operands)


def assign_kernel(tiles_ref, order_ref):
    blocks = MP * MP
    width = tiles_ref.shape[1]
    first = lax.axis_index("nodes") * blocks
    ids = tiles_ref[1:2, :] - first
    block = lax.broadcasted_iota(jnp.int32, (blocks, width), 0)
    tally = jnp.sum(jnp.where(ids == block, 1.0, 0.0), axis=1, keepdims=True)
    wide = jnp.broadcast_to(tally, (blocks, BLOCK))
    across = jnp.concatenate([wide] * (BLOCK // blocks), axis=0).T[:blocks, :blocks]
    down = wide[:, :blocks]
    i = lax.broadcasted_iota(jnp.int32, (blocks, blocks), 0)
    j = lax.broadcasted_iota(jnp.int32, (blocks, blocks), 1)
    ahead = jnp.logical_or(across > down, jnp.logical_and(across == down, j < i))
    rank = jnp.sum(jnp.where(ahead, 1.0, 0.0), axis=1, keepdims=True).astype(jnp.int32)
    device, turn = j // MP, lax.rem(j, MP)
    dealt = jnp.where(lax.rem(turn, 2) == 0, device, MP - 1 - device) + turn * MP
    chosen = jnp.where(rank == dealt, i.astype(F32), 0.0)
    order_ref[...] = jnp.sum(chosen, axis=0, keepdims=True).astype(jnp.int32)


def assign(dec_tiles):
    vmem = pl.BlockSpec(memory_space=pltpu.VMEM)
    return pl.pallas_call(
        assign_kernel,
        in_specs=[vmem],
        out_specs=vmem,
        out_shape=jax.ShapeDtypeStruct((1, MP * MP), jnp.int32),
        name="assign",
    )(dec_tiles)


def exchange_kernel(agg_hbm, wo_hbm, out_ref, agg, wo_ref, rows_ref, send, recv, fetch):
    me = lax.axis_index("mp")
    share, hid = agg_hbm.shape
    width = wo_hbm.shape[2] // MP
    blocks = share // BLOCK
    y_at = [lax.rem(me + k, MP) for k in range(MP)]
    y_from = [lax.rem(me + MP - k, MP) for k in range(MP)]

    def get(b):
        here = pl.ds(b * BLOCK, BLOCK)
        return pltpu.make_async_copy(agg_hbm.at[here], agg.at[here], fetch.at[b])

    get_wo = pltpu.make_async_copy(wo_hbm, wo_ref, fetch.at[blocks])
    get_wo.start()
    for b in range(blocks):
        get(b).start()
    barrier = pltpu.get_barrier_semaphore()
    for k in range(1, MP):
        pl.semaphore_signal(barrier, inc=1, device_id={"mp": y_at[k]}, device_id_type=MESH)
    get_wo.wait()
    wh, wl = split(wo_ref[...].reshape(hid, MP * width))

    def copy(b, k, at):
        return pltpu.make_async_remote_copy(
            src_ref=rows_ref.at[y_at[k], pl.ds(b * BLOCK, BLOCK)],
            dst_ref=out_ref.at[at * blocks + b],
            send_sem=send.at[b, k - 1],
            recv_sem=recv.at[b, k - 1],
            device_id={"mp": y_at[k]},
            device_id_type=MESH,
        )

    for b in range(blocks):
        get(b).wait()
        here = slice(b * BLOCK, (b + 1) * BLOCK)
        ah, al = split(agg[here, :])
        done = mm3(ah, al, wh, wl)
        for m in range(MP):
            rows_ref[m, here, :] = done[:, m * width : (m + 1) * width]
        if b == 0:
            pl.semaphore_wait(barrier, MP - 1)
        for k in (2, 1, 3):
            copy(b, k, me).start()
        out_ref[me * blocks + b] = rows_ref[me, here, :]
    for b in range(blocks):
        for k in range(1, MP):
            copy(b, k, y_from[k]).wait_recv()
            copy(b, k, me).wait_send()


def exchange(agg, dec_out_w):
    dma = pltpu.SemaphoreType.DMA
    vmem = pl.BlockSpec(memory_space=pltpu.VMEM)
    hbm = pl.BlockSpec(memory_space=pltpu.HBM)
    share, hid = agg.shape
    width = dec_out_w.shape[2] // MP
    blocks = share // BLOCK
    return pl.pallas_call(
        exchange_kernel,
        in_specs=[hbm, hbm],
        out_specs=vmem,
        out_shape=jax.ShapeDtypeStruct((MP * blocks, BLOCK, width), F32),
        scratch_shapes=[
            pltpu.VMEM((share, hid), F32),
            pltpu.VMEM(dec_out_w.shape, F32),
            pltpu.VMEM((MP, share, width), F32),
            dma((blocks, MP - 1)),
            dma((blocks, MP - 1)),
            dma((blocks + 1,)),
        ],
        compiler_params=pltpu.CompilerParams(
            collective_id=1, has_side_effects=True, vmem_limit_bytes=62 << 20
        ),
        name="exchange",
    )(agg, dec_out_w)


def finish_kernel(order, grid_hbm, rows_hbm, out_hbm, held, rows_ref, sums, sems, row_sems, out_sems):
    blocks, _, width = rows_hbm.shape
    columns = pl.ds(pl.multiple_of(lax.axis_index("mp") * width, width), width)

    def place(p):
        return pl.ds(pl.multiple_of(order[0, p] * BLOCK, BLOCK), BLOCK)

    def get(p):
        return pltpu.make_async_copy(grid_hbm.at[place(p), columns], held.at[p], sems.at[p])

    def put(p):
        return pltpu.make_async_copy(sums.at[p], out_hbm.at[place(p)], out_sems.at[p])

    def get_rows(p):
        return pltpu.make_async_copy(rows_hbm.at[p], rows_ref.at[p], row_sems.at[p])

    for p in range(blocks):
        get_rows(p).start()
        get(p).start()
    for p in range(blocks):
        get_rows(p).wait()
        get(p).wait()
        sums[p] = held[p] + rows_ref[p]
        put(p).start()
    for p in range(blocks):
        put(p).wait()


def finish(order, grid_latent, rows):
    blocks, _, width = rows.shape
    hbm = pl.BlockSpec(memory_space=pltpu.HBM)
    dma = pltpu.SemaphoreType.DMA
    return pl.pallas_call(
        finish_kernel,
        in_specs=[pl.BlockSpec(memory_space=pltpu.SMEM), hbm, hbm],
        out_specs=hbm,
        out_shape=jax.ShapeDtypeStruct((blocks * BLOCK, width), F32),
        scratch_shapes=[
            pltpu.VMEM(rows.shape, F32),
            pltpu.VMEM(rows.shape, F32),
            pltpu.VMEM(rows.shape, F32),
            dma((blocks,)),
            dma((blocks,)),
            dma((blocks,)),
        ],
        compiler_params=pltpu.CompilerParams(vmem_limit_bytes=62 << 20),
        name="finish",
    )(order, grid_latent, rows)


def decoder_kernel(
    tiles, order, edges_hbm, gcat_hbm, mesh_hbm, agg, edges_ref, gcat, mesh_ref, mcat, sems
):
    rows, hid = agg.shape
    width = mesh_hbm.shape[2]
    blocks = rows // BLOCK
    node = lax.axis_index("nodes")
    nodes = lax.axis_size("nodes")
    me = lax.axis_index("mp")
    first = node * MP * blocks
    fetch_mesh = pltpu.make_async_copy(mesh_hbm, mesh_ref, sems.at[0])
    fetch_mesh.start()
    fetch_edges = pltpu.make_async_copy(edges_hbm, edges_ref, sems.at[1])
    fetch_edges.start()
    fetch_gcat = pltpu.make_async_copy(gcat_hbm, gcat, sems.at[2])
    fetch_gcat.start()
    agg[...] = jnp.zeros_like(agg)
    mine = [order[0, me * blocks + s] for s in range(blocks)]
    fetch_mesh.wait()
    high, low = split(mesh_ref[...].reshape(-1, width))
    mcat[:, :hid] = high
    mcat[:, hid:] = low
    fetch_edges.wait()
    fetch_gcat.wait()

    def body(t, carry):
        block = tiles[1, t] - first
        spot = jnp.int32(-1)
        for s in range(blocks):
            spot = jnp.where(block == mine[s], s, spot)

        @pl.when(spot >= 0)
        def _():
            beside = lax.rem(tiles[0, t] - (node - 1) + nodes, nodes)
            ids = edges_ref[t]
            hot = one_hot_cols(ids[1:2])
            picked = jnp.concatenate([one_hot_cols(ids[0:1]), hot], axis=0)
            here = pl.ds(pl.multiple_of(spot * BLOCK, BLOCK), BLOCK)
            there = pl.ds(pl.multiple_of(beside * BLOCK, BLOCK), BLOCK)
            table = jnp.concatenate([mcat[there, :], gcat[here, :]], axis=0)
            pre = mm_first(picked, table)
            mh, ml = split(silu(pre[:, :hid] + pre[:, hid:]))
            agg[here, :] += mm(hot, mh) + mm(hot, ml)

        return carry

    lax.fori_loop(0, edges_ref.shape[0], body, 0)


def decoder(gdec, mesh_beside, dec_tiles, dec_edges, order):
    share, hid = gdec.shape[0], gdec.shape[1] // 2
    smem = pl.BlockSpec(memory_space=pltpu.SMEM)
    hbm = pl.BlockSpec(memory_space=pltpu.HBM)
    return pl.pallas_call(
        decoder_kernel,
        in_specs=[smem, smem, hbm, hbm, hbm],
        out_specs=pl.BlockSpec(memory_space=pltpu.VMEM),
        out_shape=jax.ShapeDtypeStruct((share, hid), F32),
        scratch_shapes=[
            pltpu.VMEM(dec_edges.shape, jnp.int32),
            pltpu.VMEM(gdec.shape, BF16),
            pltpu.VMEM(mesh_beside.shape, F32),
            pltpu.VMEM((3 * BLOCK, 2 * hid), BF16),
            pltpu.SemaphoreType.DMA((3,)),
        ],
        compiler_params=pltpu.CompilerParams(vmem_limit_bytes=62 << 20),
        name="decoder",
    )(dec_tiles, order, dec_edges, gdec, mesh_beside)


def per_device(
    grid_latent,
    mesh_latent,
    enc_grid_w,
    enc_mesh_w,
    enc_out_w,
    block_gain,
    query_w,
    key_w,
    value_w,
    out_w,
    up_w,
    down_w,
    dec_gain,
    dec_grid_w,
    dec_mesh_w,
    dec_out_w,
    neighbor_blocks,
    enc_tiles,
    enc_edges,
    dec_tiles,
    dec_edges,
):
    arrays = dict(
        enc_grid_w=enc_grid_w,
        mesh_latent=mesh_latent,
        enc_mesh_w=enc_mesh_w,
        enc_edges=enc_edges,
        enc_out_w=enc_out_w,
        block_gain=block_gain[None],
        query_w=query_w,
        key_w=key_w,
        value_w=value_w,
        out_w=out_w,
        up_w=up_w,
        down_w=down_w,
        dec_gain=dec_gain[None],
        dec_grid_w=dec_grid_w,
        dec_mesh_w=dec_mesh_w,
        dec_out_w=dec_out_w,
    )
    order = assign(dec_tiles.T)
    beside, gdec, dec_out_all = mesh_part(
        enc_tiles.T, neighbor_blocks.T, order, grid_latent, arrays
    )
    agg = decoder(gdec, beside, dec_tiles.T, dec_edges, order)
    return finish(order, grid_latent, exchange(agg, dec_out_all))


def solution(mesh):
    in_specs = (
        P("nodes", None),
        P("nodes", None),
        P(None, "mp"),
        P(None, "mp"),
        P("mp", None),
        P(),
        P(None, "mp"),
        P(None, "mp"),
        P(None, "mp"),
        P("mp", None),
        P(None, "mp"),
        P("mp", None),
        P(),
        P(None, "mp"),
        P(None, "mp"),
        P("mp", None),
        P(),
        P("nodes", None),
        P("nodes", None, None),
        P("nodes", None),
        P("nodes", None, None),
    )
    out_specs = P("nodes", "mp")
    return jax.shard_map(
        per_device, mesh=mesh, in_specs=in_specs, out_specs=out_specs, check_vma=False
    )
```

time: 129 us -> 104 us (0.81)
  local copies, waits for them, and re-layouts: 19.2 us -> 0 us
  Pallas kernels: 109 us -> 103 us
    unnamed x34 -> x0, local copies, waits for them, and re-layouts: 17.9 us -> none
    pallas_call x3 -> x5, Pallas kernels: 109 us -> 103 us  [the longest x1 72.4 us: mesh_part(): pl.pallas_call(mesh_kernel, in_specs=[smem, smem, smem, hbm] + [hbm] * le...]
    dynamic_slice x1 -> x0, local copies, waits for them, and re-layouts: 1.29 us -> none  [decoder(): mine = lax.dynamic_slice_in_dim(grid_latent, me * share, share, 0)]
where the time goes in v3:
time: 104 us; the launch traced here: 103 us
  Pallas kernels  103 us (99%)
    pallas_call x1, Pallas kernels, mesh_part(): pl.pallas_call(mesh_kernel, in_specs=[smem, smem, smem, hbm] + [hbm] * le...  72.4 us
    pallas_call x1, Pallas kernels, exchange(): pl.pallas_call(exchange_kernel, in_specs=[hbm, hbm], out_specs=vmem, out_...  16.3 us
    pallas_call x1, Pallas kernels, decoder(): pl.pallas_call(decoder_kernel, in_specs=[smem, smem, hbm, hbm, hbm], out_...  10 us
    pallas_call x1, Pallas kernels, finish(): pl.pallas_call(finish_kernel, in_specs=[pl.BlockSpec(memory_space=pltpu.S...  3.3 us

profile of v3, /device:TPU:3, one launch (start us, length us, event | category | flops | bytes accessed | tf_op | source)
XLA Modules:
  0.0 103.4 jit_solution(8183833421081563114)
XLA Ops:
  0.0 1.4 %assign.1.order = s32[1,16]{1,0:T(1,128)} custom-call(s32[2,48]{1,0:T(2,128)} %bitcast.8), custom_call_target="tpu_custom_call" | custom-call | tf_op jit(solution)/shard_map/assign/pallas_call | solution.py:606
  1.4 72.4 %mesh_part.1 = (f32[3,128,512]{2,1,0:T(8,128)}, bf16[512,1024]{1,0:T(8,128)(2,1)}, f32[4,128,512]{2,1,0:T(8,128)}) custom-call(s32[2,32]{1,0:T(2,128)} %bitcast.10, s32[16,64]{1,0:T(8,128)} %bitcast.5, s32[1,16]{1,0:T(1,128)} %assign.1.order, f32[2048,512]{1,0:T(8,128)} %grid_hbm.3, f32[512,128]{1,0:T(8,128)} %refs_0_.1, f32[128,512]{1,0:T(8,128)} %refs_1_.1, ...), custom_call_target="tpu_custom_call" | custom-call | tf_op jit(solution)/shard_map/mesh_part/pallas_call | solution.py:537
  73.8 10.0 %decoder.1.agg_hbm = f32[512,512]{1,0:T(8,128)} custom-call(s32[2,48]{1,0:T(2,128)} %bitcast.9, s32[1,16]{1,0:T(1,128)} %assign.1.order, s32[48,2,128]{2,1,0:T(2,128)} %edges_hbm.1, bf16[512,1024]{1,0:T(8,128)(2,1)} %get-tuple-element.8.gcat_hbm, f32[3,128,512]{2,1,0:T(8,128)} %get-tuple-element.9.mesh_hbm), custom_call_target="tpu_custom_call" | custom-call | tf_op jit(solution)/shard_map/decoder/pallas_call | solution.py:795
  83.8 16.3 %exchange.1.rows_hbm = f32[16,128,128]{2,1,0:T(8,128)} custom-call(f32[512,512]{1,0:T(8,128)} %decoder.1.agg_hbm, f32[4,128,512]{2,1,0:T(8,128)} %get-tuple-element.10.wo_hbm), custom_call_target="tpu_custom_call" | custom-call | tf_op jit(solution)/shard_map/exchange/pallas_call | solution.py:672
  100.1 3.3 %finish.1 = f32[2048,128]{1,0:T(8,128)} custom-call(s32[1,16]{1,0:T(1,128)} %assign.1.order, f32[2048,512]{1,0:T(8,128)} %grid_hbm.3, f32[16,128,128]{2,1,0:T(8,128)} %exchange.1.rows_hbm), custom_call_target="tpu_custom_call" | custom-call | tf_op jit(solution)/shard_map/finish/pallas_call | solution.py:724

commit v4 on v3

--- a/solution.py
+++ b/solution.py
@@ -159,6 +159,8 @@
         summed,
         att_all,
         scores,
+        out_cat,
+        dec_cat,
         fetch_sem,
         grid_sem,
         y_send,
@@ -326,13 +328,13 @@
             live = tile >= 0
             block = jnp.clip(tile - first, 0, blocks - 1)
             ids = enc_edges[t]
-            target = one_hot_cols(ids[1:2])
+            target = one_hot_cols(jnp.where(live, ids[1:2], -1))
             picked = jnp.concatenate([one_hot_cols(ids[0:1]), target], axis=0)
             table = jnp.concatenate([gcat[block], mcat[...]], axis=0)
             pre = mm_first(picked, table)
             mh, ml = split(silu(pre[:, :hid] + pre[:, hid:]))
             messages.append(jnp.concatenate([mh, ml], axis=1))
-            hots.append(one_hot_cols(jnp.where(live, ids[1:2], -1)))
+            hots.append(target)
         acc[...] += mm(jnp.concatenate(hots, axis=1), jnp.concatenate(messages, axis=0))
         return carry
 
@@ -454,7 +456,14 @@
     for k in range(1, MP):
         y_copy(7, k, summed.at[share_of(me)], summed.at[share_of(y_from[k])]).wait_recv()
     mesh_mid = mesh_one + summed[...]
-    weight_finish(2)
+    for item, whole in ((2, out_cat), (3, dec_cat)):
+        weight_finish(item)
+        if item == 2:
+            high, low = split(out_all[...].reshape(width, width))
+        else:
+            high, low = split(jnp.concatenate([dec_mesh_all[m] for m in range(MP)], axis=1))
+        whole[:, :width] = high
+        whole[:, width:] = low
     core_copy(kv.at[pl.ds((1 - core) * CHIPS, CHIPS)]).wait_recv()
 
     count = lists.shape[0]
@@ -481,14 +490,12 @@
     att_all[me] = mm3(wh, wl, vh, vl) / total
     for k in range(1, MP):
         y_copy(8, k, att_all.at[me], att_all.at[me]).start()
-    weight_finish(3)
     for k in range(1, MP):
         y_copy(8, k, att_all.at[me], att_all.at[y_from[k]]).wait_recv()
     attended = jnp.concatenate([att_all[m] for m in range(MP)], axis=1)
-    mesh_two = mesh_mid + mm3(*split(attended), *split(out_all[...].reshape(width, width)))
+    mesh_two = mesh_mid + mm3(*split(attended), out_cat[:, :width], out_cat[:, width:])
     normed_two = norm_rows(mesh_two, got("dec_gain"))
-    dec_w = jnp.concatenate([dec_mesh_all[m] for m in range(MP)], axis=1)
-    beside[1] = mm3(*split(normed_two), *split(dec_w))
+    beside[1] = mm3(*split(normed_two), dec_cat[:, :width], dec_cat[:, width:])
 
     def side_copy(way, slot, target):
         return pltpu.make_async_remote_copy(
@@ -561,6 +568,8 @@
             pltpu.VMEM((nodes, width), F32),
             pltpu.VMEM((MP, nodes, HEAD_DIM), F32),
             pltpu.VMEM((nodes, listed * BLOCK), F32),
+            pltpu.VMEM((width, 2 * width), BF16),
+            pltpu.VMEM((width, 2 * width), BF16),
             dma((len(operands),)),
             dma((rows // 256,)),
             dma((9, MP - 1)),
@@ -740,7 +749,7 @@
 
 
 def decoder_kernel(
-    tiles, order, edges_hbm, gcat_hbm, mesh_hbm, agg, edges_ref, gcat, mesh_ref, mcat, sems
+    tiles, order, edges_hbm, gcat_hbm, mesh_hbm, agg, edges_ref, gcat, mesh_ref, mcat, todo, sems
 ):
     rows, hid = agg.shape
     width = mesh_hbm.shape[2]
@@ -749,6 +758,7 @@
     nodes = lax.axis_size("nodes")
     me = lax.axis_index("mp")
     first = node * MP * blocks
+    group = 2
     fetch_mesh = pltpu.make_async_copy(mesh_hbm, mesh_ref, sems.at[0])
     fetch_mesh.start()
     fetch_edges = pltpu.make_async_copy(edges_hbm, edges_ref, sems.at[1])
@@ -764,28 +774,37 @@
     fetch_edges.wait()
     fetch_gcat.wait()
 
-    def body(t, carry):
+    def pick(t, found):
         block = tiles[1, t] - first
         spot = jnp.int32(-1)
         for s in range(blocks):
             spot = jnp.where(block == mine[s], s, spot)
-
-        @pl.when(spot >= 0)
-        def _():
+        todo[0, found] = t
+        todo[1, found] = spot
+        return found + jnp.where(spot >= 0, 1, 0)
+
+    found = lax.fori_loop(0, edges_ref.shape[0], pick, jnp.int32(0))
+    for k in range(group):
+        todo[0, found + k] = 0
+        todo[1, found + k] = -1
+
+    def body(i, carry):
+        for k in range(group):
+            t, spot = todo[0, i * group + k], todo[1, i * group + k]
+            live = spot >= 0
             beside = lax.rem(tiles[0, t] - (node - 1) + nodes, nodes)
             ids = edges_ref[t]
-            hot = one_hot_cols(ids[1:2])
+            hot = one_hot_cols(jnp.where(live, ids[1:2], -1))
             picked = jnp.concatenate([one_hot_cols(ids[0:1]), hot], axis=0)
-            here = pl.ds(pl.multiple_of(spot * BLOCK, BLOCK), BLOCK)
+            here = pl.ds(pl.multiple_of(jnp.maximum(spot, 0) * BLOCK, BLOCK), BLOCK)
             there = pl.ds(pl.multiple_of(beside * BLOCK, BLOCK), BLOCK)
             table = jnp.concatenate([mcat[there, :], gcat[here, :]], axis=0)
             pre = mm_first(picked, table)
             mh, ml = split(silu(pre[:, :hid] + pre[:, hid:]))
             agg[here, :] += mm(hot, mh) + mm(hot, ml)
-
         return carry
 
-    lax.fori_loop(0, edges_ref.shape[0], body, 0)
+    lax.fori_loop(0, (found + group - 1) // group, body, 0)
 
 
 def decoder(gdec, mesh_beside, dec_tiles, dec_edges, order):
@@ -802,6 +821,7 @@
             pltpu.VMEM(gdec.shape, BF16),
             pltpu.VMEM(mesh_beside.shape, F32),
             pltpu.VMEM((3 * BLOCK, 2 * hid), BF16),
+            pltpu.SMEM((2, dec_edges.shape[0] + 8), jnp.int32),
             pltpu.SemaphoreType.DMA((3,)),
         ],
         compiler_params=pltpu.CompilerParams(vmem_limit_bytes=62 << 20),

time: 104 us -> 103 us (level)
    pallas_call x1, Pallas kernels: 10 us -> 7.64 us  [decoder(): pl.pallas_call(decoder_kernel, in_specs=[smem, smem, hbm, hbm, hbm], out_...]
    pallas_call x1, Pallas kernels: 16.3 us -> 17.5 us  [exchange(): pl.pallas_call(exchange_kernel, in_specs=[hbm, hbm], out_specs=vmem, out_...]
where the time goes in v4:
time: 103 us; the launch traced here: 102 us
  Pallas kernels  102 us (99%)
    pallas_call x1, Pallas kernels, mesh_part(): pl.pallas_call(mesh_kernel, in_specs=[smem, smem, smem, hbm] + [hbm] * le...  72.4 us
    pallas_call x1, Pallas kernels, exchange(): pl.pallas_call(exchange_kernel, in_specs=[hbm, hbm], out_specs=vmem, out_...  17.5 us
    pallas_call x1, Pallas kernels, decoder(): pl.pallas_call(decoder_kernel, in_specs=[smem, smem, hbm, hbm, hbm], out_...  7.64 us
    pallas_call x1, Pallas kernels, finish(): pl.pallas_call(finish_kernel, in_specs=[pl.BlockSpec(memory_space=pltpu.S...  3.3 us

profile of v4, /device:TPU:3, one launch (start us, length us, event | category | flops | bytes accessed | tf_op | source)
XLA Modules:
  0.0 102.3 jit_solution(17568768542518330843)
XLA Ops:
  0.0 1.4 %assign.1.order = s32[1,16]{1,0:T(1,128)} custom-call(s32[2,48]{1,0:T(2,128)} %bitcast.8), custom_call_target="tpu_custom_call" | custom-call | tf_op jit(solution)/shard_map/assign/pallas_call | solution.py:615
  1.4 72.4 %mesh_part.1 = (f32[3,128,512]{2,1,0:T(8,128)}, bf16[512,1024]{1,0:T(8,128)(2,1)}, f32[4,128,512]{2,1,0:T(8,128)}) custom-call(s32[2,32]{1,0:T(2,128)} %bitcast.10, s32[16,64]{1,0:T(8,128)} %bitcast.5, s32[1,16]{1,0:T(1,128)} %assign.1.order, f32[2048,512]{1,0:T(8,128)} %grid_hbm.3, f32[512,128]{1,0:T(8,128)} %refs_0_.1, f32[128,512]{1,0:T(8,128)} %refs_1_.1, ...), custom_call_target="tpu_custom_call" | custom-call | tf_op jit(solution)/shard_map/mesh_part/pallas_call | solution.py:544
  73.8 7.6 %decoder.1.agg_hbm = f32[512,512]{1,0:T(8,128)} custom-call(s32[2,48]{1,0:T(2,128)} %bitcast.9, s32[1,16]{1,0:T(1,128)} %assign.1.order, s32[48,2,128]{2,1,0:T(2,128)} %edges_hbm.1, bf16[512,1024]{1,0:T(8,128)(2,1)} %get-tuple-element.8.gcat_hbm, f32[3,128,512]{2,1,0:T(8,128)} %get-tuple-element.9.mesh_hbm), custom_call_target="tpu_custom_call" | custom-call | tf_op jit(solution)/shard_map/decoder/pallas_call | solution.py:814
  81.4 17.5 %exchange.1.rows_hbm = f32[16,128,128]{2,1,0:T(8,128)} custom-call(f32[512,512]{1,0:T(8,128)} %decoder.1.agg_hbm, f32[4,128,512]{2,1,0:T(8,128)} %get-tuple-element.10.wo_hbm), custom_call_target="tpu_custom_call" | custom-call | tf_op jit(solution)/shard_map/exchange/pallas_call | solution.py:681
  99.0 3.3 %finish.1 = f32[2048,128]{1,0:T(8,128)} custom-call(s32[1,16]{1,0:T(1,128)} %assign.1.order, f32[2048,512]{1,0:T(8,128)} %grid_hbm.3, f32[16,128,128]{2,1,0:T(8,128)} %exchange.1.rows_hbm), custom_call_target="tpu_custom_call" | custom-call | tf_op jit(solution)/shard_map/finish/pallas_call | solution.py:733

commit v5 on v4

--- a/solution.py
+++ b/solution.py
@@ -495,20 +495,27 @@
     attended = jnp.concatenate([att_all[m] for m in range(MP)], axis=1)
     mesh_two = mesh_mid + mm3(*split(attended), out_cat[:, :width], out_cat[:, width:])
     normed_two = norm_rows(mesh_two, got("dec_gain"))
-    beside[1] = mm3(*split(normed_two), dec_cat[:, :width], dec_cat[:, width:])
-
-    def side_copy(way, slot, target):
+    th, tl = split(normed_two)
+    part_width = width // 2
+
+    def side_copy(way, part, slot, target):
+        columns = pl.ds(part * part_width, part_width)
         return pltpu.make_async_remote_copy(
-            src_ref=beside.at[1],
-            dst_ref=beside.at[slot],
-            send_sem=side_send.at[way],
-            recv_sem=side_recv.at[way],
+            src_ref=beside.at[1, :, columns],
+            dst_ref=beside.at[slot, :, columns],
+            send_sem=side_send.at[way, part],
+            recv_sem=side_recv.at[way, part],
             device_id={"nodes": target},
             device_id_type=MESH,
         )
 
-    side_copy(0, 0, after).start()
-    side_copy(1, 2, before).start()
+    for part in range(2):
+        low, high = part * part_width, (part + 1) * part_width
+        beside[1, :, low:high] = mm3(
+            th, tl, dec_cat[:, low:high], dec_cat[:, width + low : width + high]
+        )
+        side_copy(0, part, 0, after).start()
+        side_copy(1, part, 2, before).start()
     weight_finish(4)
     core_copy(kv.at[pl.ds(core * CHIPS, CHIPS)]).wait_send()
     link_copy_all = pltpu.make_async_remote_copy(
@@ -527,8 +534,9 @@
         for k in range(1, MP):
             ref = summed.at[share_of(me)]
             y_copy(item, k, ref, ref).wait_send()
-    side_copy(0, 0, after).wait()
-    side_copy(1, 2, before).wait()
+    for part in range(2):
+        side_copy(0, part, 0, after).wait()
+        side_copy(1, part, 2, before).wait()
 
 
 def mesh_part(tiles, lists, order, grid_latent, arrays):
@@ -580,8 +588,8 @@
             dma((len(CHUNKS), CHIPS)),
             dma(()),
             dma(()),
-            dma((2,)),
-            dma((2,)),
+            dma((2, 2)),
+            dma((2, 2)),
         ],
         compiler_params=pltpu.CompilerParams(
             collective_id=0, has_side_effects=True, vmem_limit_bytes=62 << 20

time: 103 us -> 102 us (level)
  Pallas kernels: 102 us -> 100 us
    pallas_call x1, Pallas kernels: 17.5 us -> 14.9 us  [exchange(): pl.pallas_call(exchange_kernel, in_specs=[hbm, hbm], out_specs=vmem, out_...]
where the time goes in v5:
time: 102 us; the launch traced here: 100 us
  Pallas kernels  100 us (98%)
    pallas_call x1, Pallas kernels, mesh_part(): pl.pallas_call(mesh_kernel, in_specs=[smem, smem, smem, hbm] + [hbm] * le...  72.4 us
    pallas_call x1, Pallas kernels, exchange(): pl.pallas_call(exchange_kernel, in_specs=[hbm, hbm], out_specs=vmem, out_...  14.9 us
    pallas_call x1, Pallas kernels, decoder(): pl.pallas_call(decoder_kernel, in_specs=[smem, smem, hbm, hbm, hbm], out_...  8.46 us
    pallas_call x1, Pallas kernels, finish(): pl.pallas_call(finish_kernel, in_specs=[pl.BlockSpec(memory_space=pltpu.S...  3.3 us

profile of v5, /device:TPU:3, one launch (start us, length us, event | category | flops | bytes accessed | tf_op | source)
XLA Modules:
  0.0 100.5 jit_solution(15469769891176106680)
XLA Ops:
  0.0 1.4 %assign.1.order = s32[1,16]{1,0:T(1,128)} custom-call(s32[2,48]{1,0:T(2,128)} %bitcast.8), custom_call_target="tpu_custom_call" | custom-call | tf_op jit(solution)/shard_map/assign/pallas_call | solution.py:623
  1.4 72.4 %mesh_part.1 = (f32[3,128,512]{2,1,0:T(8,128)}, bf16[512,1024]{1,0:T(8,128)(2,1)}, f32[4,128,512]{2,1,0:T(8,128)}) custom-call(s32[2,32]{1,0:T(2,128)} %bitcast.10, s32[16,64]{1,0:T(8,128)} %bitcast.5, s32[1,16]{1,0:T(1,128)} %assign.1.order, f32[2048,512]{1,0:T(8,128)} %grid_hbm.3, f32[512,128]{1,0:T(8,128)} %refs_0_.1, f32[128,512]{1,0:T(8,128)} %refs_1_.1, ...), custom_call_target="tpu_custom_call" | custom-call | tf_op jit(solution)/shard_map/mesh_part/pallas_call | solution.py:552
  73.8 8.5 %decoder.1.agg_hbm = f32[512,512]{1,0:T(8,128)} custom-call(s32[2,48]{1,0:T(2,128)} %bitcast.9, s32[1,16]{1,0:T(1,128)} %assign.1.order, s32[48,2,128]{2,1,0:T(2,128)} %edges_hbm.1, bf16[512,1024]{1,0:T(8,128)(2,1)} %get-tuple-element.8.gcat_hbm, f32[3,128,512]{2,1,0:T(8,128)} %get-tuple-element.9.mesh_hbm), custom_call_target="tpu_custom_call" | custom-call | tf_op jit(solution)/shard_map/decoder/pallas_call | solution.py:822
  82.3 14.9 %exchange.1.rows_hbm = f32[16,128,128]{2,1,0:T(8,128)} custom-call(f32[512,512]{1,0:T(8,128)} %decoder.1.agg_hbm, f32[4,128,512]{2,1,0:T(8,128)} %get-tuple-element.10.wo_hbm), custom_call_target="tpu_custom_call" | custom-call | tf_op jit(solution)/shard_map/exchange/pallas_call | solution.py:689
  97.2 3.3 %finish.1 = f32[2048,128]{1,0:T(8,128)} custom-call(s32[1,16]{1,0:T(1,128)} %assign.1.order, f32[2048,512]{1,0:T(8,128)} %grid_hbm.3, f32[16,128,128]{2,1,0:T(8,128)} %exchange.1.rows_hbm), custom_call_target="tpu_custom_call" | custom-call | tf_op jit(solution)/shard_map/finish/pallas_call | solution.py:741
